TPU v7x, 32 devices: a whole 2x2x4 slice. The times are simulated.
32 devices in a mesh: section: 2 (over y), dp: 16 (over z, x, core).
Axes of the slice: x: 2, y: 2, z: 4, core: 2. Of those that a mesh axis runs over, the one named last changes fastest.
Arguments:
- boundary: bfloat16 [2, 2, 2048, 960], P('section', None, 'dp'), may hold values from -6 to 6
- doc_lens: int32 [2, 16, 4], P(None, 'dp'), may hold values from 0 to 128, as said below
- w_query: bfloat16 [2, 921600], P('section', 'dp'), may hold values from -0.1875 to 0.1875
- w_key: bfloat16 [2, 307200], P('section', 'dp'), may hold values from -0.1875 to 0.1875
- w_value: bfloat16 [2, 307200], P('section', 'dp'), may hold values from -0.1875 to 0.1875
- w_out: bfloat16 [2, 921600], P('section', 'dp'), may hold values from -0.75 to 0.75
- gains: bfloat16 [2, 1920], P('section', 'dp'), may hold values from 0.5 to 1.5
- w_gate: bfloat16 [2, 2457600], P('section', 'dp'), may hold values from -0.1875 to 0.1875
- w_up: bfloat16 [2, 2457600], P('section', 'dp'), may hold values from -0.1875 to 0.1875
- w_down: bfloat16 [2, 2457600], P('section', 'dp'), may hold values from -0.125 to 0.125
Outputs:
- boundary_out: float32 [2, 2, 2048, 960], P('section', None, 'dp')
- grad_query: float32 [2, 921600], P('section', 'dp')
- grad_key: float32 [2, 307200], P('section', 'dp')
- grad_value: float32 [2, 307200], P('section', 'dp')
- grad_out: float32 [2, 921600], P('section', 'dp')
- grad_gains: float32 [2, 1920], P('section', 'dp')
- grad_gate: float32 [2, 2457600], P('section', 'dp')
- grad_up: float32 [2, 2457600], P('section', 'dp')
- grad_down: float32 [2, 2457600], P('section', 'dp')
Inputs may be any that keep to these rules, and one draw needn't show every extreme that they name: `doc_lens`: in each micro-batch and group of 128 slots the 4 lengths sum to at most 128; documents fill the slots from the first in order and the rest is padding. In every micro-batch one group holds a single document of 128.
All inputs are finite; a program needn't handle non-finite values.
Results may differ from a plain program's by a relative error of at most 0.02.
Values may be sent and summed in bfloat16 or wider, within the bound.
A program may use at most 256 MiB of HBM per device.

v0:
```python
import jax
import jax.numpy as jnp
from jax import lax
from jax.sharding import PartitionSpec as P

HEAD = 64


EPSILON = 1e-05
ROPE_BASE = 100000.0


def passed_along(x, axis, by):
    devices = lax.axis_size(axis)
    pairs = [(i, i + by) for i in range(devices) if 0 <= i + by < devices]
    return lax.ppermute(x, axis, pairs)


def as_sent(x):
    return jax.tree.map(lambda a: a.astype(jnp.bfloat16) if a.dtype == jnp.float32 else a, x)


def doc_layout(lengths, slot_count):
    doc_ends = jnp.cumsum(lengths, dtype=jnp.int32)
    doc_starts = doc_ends - lengths
    doc_count = lengths.shape[0]
    slot_ids = jnp.arange(slot_count, dtype=jnp.int32)
    segment = jnp.sum(
        (slot_ids[:, None] >= doc_ends[None, :]).astype(jnp.int32), axis=1, dtype=jnp.int32
    )
    start_table = jnp.concatenate([doc_starts, doc_ends[doc_count - 1 :]])
    picked = segment[:, None] == jnp.arange(doc_count + 1, dtype=jnp.int32)[None, :]
    first_slot = jnp.sum(jnp.where(picked, start_table[None, :], 0), axis=1, dtype=jnp.int32)
    return (segment, slot_ids - first_slot, segment < doc_count)


def rope_tables(position):
    half_width = HEAD // 2
    inverse_freq = ROPE_BASE ** (-(jnp.arange(half_width, dtype=jnp.float32) * (2.0 / HEAD)))
    angles = position.astype(jnp.float32)[:, None] * inverse_freq[None, :]
    cos_table = jnp.cos(angles)
    sine_table = jnp.sin(angles)
    return (
        jnp.concatenate([cos_table, cos_table], axis=1),
        jnp.concatenate([sine_table, sine_table], axis=1),
    )


def rotate(values, cos_table, sine_table):
    half_width = values.shape[-1] // 2
    turned = jnp.concatenate([-values[..., half_width:], values[..., :half_width]], axis=-1)
    return values * cos_table[:, None, :] + turned * sine_table[:, None, :]


def unrotate(values, cos_table, sine_table):
    half_width = values.shape[-1] // 2
    sined = values * sine_table[:, None, :]
    turned = jnp.concatenate([sined[..., half_width:], -sined[..., :half_width]], axis=-1)
    return values * cos_table[:, None, :] + turned


def unpack(gathered, model_width):
    kv_width = gathered[1].size // model_width
    hidden_width = gathered[5].size // model_width
    return (
        gathered[0].reshape(model_width, model_width),
        gathered[1].reshape(model_width, kv_width),
        gathered[2].reshape(model_width, kv_width),
        gathered[3].reshape(model_width, model_width),
        gathered[4].reshape(2 * model_width),
        gathered[5].reshape(model_width, hidden_width),
        gathered[6].reshape(model_width, hidden_width),
        gathered[7].reshape(hidden_width, model_width),
    )


def add_sources(received):
    return tuple((jnp.sum(member, axis=0, keepdims=True) for member in received))


def forward_layer(layer_input_rows, matrices, allowed, cos_table, sine_table):
    w_query, w_key, w_value, w_out, gain_pair, w_gate, w_up, w_down = matrices
    row_count, model_width = layer_input_rows.shape
    kv_count = w_key.shape[1] // HEAD
    group_size = w_query.shape[1] // w_key.shape[1]
    score_scale = HEAD ** (-0.5)
    gain_one = gain_pair[:model_width].astype(jnp.float32)
    gain_two = gain_pair[model_width:].astype(jnp.float32)
    residual = layer_input_rows.astype(jnp.float32)
    first_inverse_scale = lax.rsqrt(jnp.mean(residual * residual, axis=1, keepdims=True) + EPSILON)
    normed = (residual * first_inverse_scale * gain_one).astype(jnp.bfloat16)
    queries = rotate(
        jnp.dot(normed, w_query, preferred_element_type=jnp.float32).reshape(row_count, -1, HEAD),
        cos_table,
        sine_table,
    ).astype(jnp.bfloat16)
    keys_turned = rotate(
        jnp.dot(normed, w_key, preferred_element_type=jnp.float32).reshape(
            row_count, kv_count, HEAD
        ),
        cos_table,
        sine_table,
    ).astype(jnp.bfloat16)
    values_low = jnp.dot(normed, w_value, preferred_element_type=jnp.float32).astype(jnp.bfloat16)
    heads_query = queries.reshape(row_count, kv_count, group_size, HEAD).transpose(1, 0, 2, 3)
    heads_key = keys_turned.transpose(1, 0, 2)
    heads_value = values_low.reshape(row_count, kv_count, HEAD).transpose(1, 0, 2)

    def one_head(operands):
        head_query, head_key, head_value = operands
        scores = (
            jnp.einsum("qgd,td->gqt", head_query, head_key, preferred_element_type=jnp.float32)
            * score_scale
        )
        scores = jnp.where(allowed[None], scores, -1e30)
        row_top = jnp.max(scores, axis=2, keepdims=True)
        exponent = jnp.exp(scores - row_top)
        row_total = jnp.sum(exponent, axis=2, keepdims=True)
        probability = (exponent / row_total).astype(jnp.bfloat16)
        attended = jnp.einsum(
            "gqt,td->qgd", probability, head_value, preferred_element_type=jnp.float32
        )
        return (attended, (row_top + jnp.log(row_total))[..., 0])

    attended, log_total = lax.map(one_head, (heads_query, heads_key, heads_value))
    mixed_low = attended.transpose(1, 0, 2, 3).reshape(row_count, model_width).astype(jnp.bfloat16)
    midway_hidden = residual + jnp.dot(mixed_low, w_out, preferred_element_type=jnp.float32)
    second_inverse_scale = lax.rsqrt(
        jnp.mean(midway_hidden * midway_hidden, axis=1, keepdims=True) + EPSILON
    )
    normed_two = (midway_hidden * second_inverse_scale * gain_two).astype(jnp.bfloat16)
    gate_pre = jnp.dot(normed_two, w_gate, preferred_element_type=jnp.float32)
    up_pre = jnp.dot(normed_two, w_up, preferred_element_type=jnp.float32)
    activation = (jax.nn.silu(gate_pre) * up_pre).astype(jnp.bfloat16)
    layer_out = midway_hidden + jnp.dot(activation, w_down, preferred_element_type=jnp.float32)
    kept_values = (
        layer_input_rows,
        normed,
        queries,
        keys_turned,
        values_low,
        log_total,
        mixed_low,
        midway_hidden,
        first_inverse_scale,
        second_inverse_scale,
        normed_two,
        gate_pre,
        up_pre,
        activation,
    )
    return (layer_out, kept_values)


def backward_layer(kept_values, matrices, allowed, cos_table, sine_table, grad_output, piece_count):
    (
        layer_input_rows,
        normed,
        queries,
        keys_turned,
        values_low,
        log_total,
        mixed_low,
        midway_hidden,
        first_inverse_scale,
        second_inverse_scale,
        normed_two,
        gate_pre,
        up_pre,
        activation,
    ) = kept_values
    w_query, w_key, w_value, w_out, gain_pair, w_gate, w_up, w_down = matrices
    row_count, model_width = layer_input_rows.shape
    kv_count = w_key.shape[1] // HEAD
    group_size = w_query.shape[1] // w_key.shape[1]
    score_scale = HEAD ** (-0.5)
    gain_one = gain_pair[:model_width].astype(jnp.float32)
    gain_two = gain_pair[model_width:].astype(jnp.float32)
    grad_low = grad_output.astype(jnp.bfloat16)
    grad_wdown = jnp.einsum("nf,nd->fd", activation, grad_low, preferred_element_type=jnp.float32)
    grad_act = jnp.einsum("nd,fd->nf", grad_low, w_down, preferred_element_type=jnp.float32)
    sigmoid_gate = jax.nn.sigmoid(gate_pre)
    grad_gate_pre = (
        grad_act * up_pre * sigmoid_gate * (1.0 + gate_pre * (1.0 - sigmoid_gate))
    ).astype(jnp.bfloat16)
    grad_up_pre = (grad_act * gate_pre * sigmoid_gate).astype(jnp.bfloat16)
    grad_wgate = jnp.einsum(
        "nd,nf->df", normed_two, grad_gate_pre, preferred_element_type=jnp.float32
    )
    grad_wup = jnp.einsum("nd,nf->df", normed_two, grad_up_pre, preferred_element_type=jnp.float32)
    second_norm_gradient = jnp.einsum(
        "nf,df->nd", grad_gate_pre, w_gate, preferred_element_type=jnp.float32
    ) + jnp.einsum("nf,df->nd", grad_up_pre, w_up, preferred_element_type=jnp.float32)
    second_centered_input = midway_hidden * second_inverse_scale
    second_normalized_rows = second_norm_gradient * gain_two
    second_gain_gradient = jnp.sum(second_norm_gradient * second_centered_input, axis=0)
    grad_middle = grad_output + second_inverse_scale * (
        second_normalized_rows
        - second_centered_input
        * jnp.mean(second_normalized_rows * second_centered_input, axis=1, keepdims=True)
    )
    grad_branch = grad_middle.astype(jnp.bfloat16)
    grad_wout = jnp.einsum("nd,ne->de", mixed_low, grad_branch, preferred_element_type=jnp.float32)
    grad_mixed = jnp.einsum(
        "ne,de->nd", grad_branch, w_out, preferred_element_type=jnp.float32
    ).astype(jnp.bfloat16)
    heads_query = queries.reshape(row_count, kv_count, group_size, HEAD).transpose(1, 0, 2, 3)
    heads_key = keys_turned.transpose(1, 0, 2)
    heads_value = values_low.reshape(row_count, kv_count, HEAD).transpose(1, 0, 2)
    heads_grad = grad_mixed.reshape(row_count, kv_count, group_size, HEAD).transpose(1, 0, 2, 3)

    def one_back(operands):
        head_query, head_key, head_value, head_lse, head_grad = operands
        scores = (
            jnp.einsum("qgd,td->gqt", head_query, head_key, preferred_element_type=jnp.float32)
            * score_scale
        )
        scores = jnp.where(allowed[None], scores, -1e30)
        probability = jnp.exp(scores - head_lse[..., None])
        grad_vhead = jnp.einsum(
            "gqt,qgd->td",
            probability.astype(jnp.bfloat16),
            head_grad,
            preferred_element_type=jnp.float32,
        )
        grad_prob = jnp.einsum(
            "qgd,td->gqt", head_grad, head_value, preferred_element_type=jnp.float32
        )
        grad_scores = (
            probability * (grad_prob - jnp.sum(probability * grad_prob, axis=2, keepdims=True))
        ).astype(jnp.bfloat16)
        grad_qhead = (
            jnp.einsum("gqt,td->qgd", grad_scores, head_key, preferred_element_type=jnp.float32)
            * score_scale
        )
        grad_khead = (
            jnp.einsum("gqt,qgd->td", grad_scores, head_query, preferred_element_type=jnp.float32)
            * score_scale
        )
        return (grad_qhead, grad_khead, grad_vhead)

    grad_qheads, grad_kheads, grad_vheads = lax.map(
        one_back, (heads_query, heads_key, heads_value, log_total, heads_grad)
    )
    grad_queries = (
        unrotate(
            grad_qheads.transpose(1, 0, 2, 3).reshape(row_count, -1, HEAD), cos_table, sine_table
        )
        .reshape(row_count, -1)
        .astype(jnp.bfloat16)
    )
    grad_keys = (
        unrotate(grad_kheads.transpose(1, 0, 2), cos_table, sine_table)
        .reshape(row_count, -1)
        .astype(jnp.bfloat16)
    )
    grad_values = grad_vheads.transpose(1, 0, 2).reshape(row_count, -1).astype(jnp.bfloat16)
    grad_wquery = jnp.einsum("nd,ne->de", normed, grad_queries, preferred_element_type=jnp.float32)
    grad_wkey = jnp.einsum("nd,ne->de", normed, grad_keys, preferred_element_type=jnp.float32)
    grad_wvalue = jnp.einsum("nd,ne->de", normed, grad_values, preferred_element_type=jnp.float32)
    first_norm_gradient = (
        jnp.einsum("ne,de->nd", grad_queries, w_query, preferred_element_type=jnp.float32)
        + jnp.einsum("ne,de->nd", grad_keys, w_key, preferred_element_type=jnp.float32)
        + jnp.einsum("ne,de->nd", grad_values, w_value, preferred_element_type=jnp.float32)
    )
    first_centered_input = layer_input_rows.astype(jnp.float32) * first_inverse_scale
    first_normalized_rows = first_norm_gradient * gain_one
    first_gain_gradient = jnp.sum(first_norm_gradient * first_centered_input, axis=0)
    grad_input = grad_middle + first_inverse_scale * (
        first_normalized_rows
        - first_centered_input
        * jnp.mean(first_normalized_rows * first_centered_input, axis=1, keepdims=True)
    )
    grad_terms = (
        grad_wquery,
        grad_wkey,
        grad_wvalue,
        grad_wout,
        jnp.concatenate([first_gain_gradient, second_gain_gradient]),
        grad_wgate,
        grad_wup,
        grad_wdown,
    )
    return (grad_input, tuple((member.reshape(piece_count, -1) for member in grad_terms)))


def on_device(boundary, doc_lens, w_query, w_key, w_value, w_out, gains, w_gate, w_up, w_down):
    sections = lax.axis_size("section")
    section_index = lax.axis_index("section")
    dp_count = lax.axis_size("dp")
    micro_count = boundary.shape[1]
    row_count = boundary.shape[2]
    model_width = boundary.shape[3]
    round_total = micro_count + sections - 1
    shards = (w_query, w_key, w_value, w_out, gains, w_gate, w_up, w_down)
    layouts = [
        doc_layout(doc_lens[micro_number, 0], row_count) for micro_number in range(micro_count)
    ]
    segments = jnp.stack([layout_item[0] for layout_item in layouts])
    positions = jnp.stack([layout_item[1] for layout_item in layouts])
    live_rows = jnp.stack([layout_item[2] for layout_item in layouts]).astype(jnp.float32)
    slot_ids = jnp.arange(row_count, dtype=jnp.int32)
    causal = slot_ids[None, :] <= slot_ids[:, None]

    def layout_for(micro_slot):
        segment = lax.dynamic_index_in_dim(segments, micro_slot, 0, keepdims=False)
        position = lax.dynamic_index_in_dim(positions, micro_slot, 0, keepdims=False)
        allowed = causal & (segment[:, None] == segment[None, :])
        cos_table, sine_table = rope_tables(position)
        return (allowed, cos_table, sine_table)

    matrices = unpack(
        (
            lax.all_gather(shards[0], "dp", axis=0, tiled=True),
            lax.all_gather(shards[1], "dp", axis=0, tiled=True),
            lax.all_gather(shards[2], "dp", axis=0, tiled=True),
            lax.all_gather(shards[3], "dp", axis=0, tiled=True),
            lax.all_gather(shards[4], "dp", axis=0, tiled=True),
            lax.all_gather(shards[5], "dp", axis=0, tiled=True),
            lax.all_gather(shards[6], "dp", axis=0, tiled=True),
            lax.all_gather(shards[7], "dp", axis=0, tiled=True),
        ),
        model_width,
    )
    own_inputs = boundary[0]
    results = jnp.zeros((micro_count, row_count, model_width), jnp.float32)
    outgoing = jnp.zeros((row_count, model_width), jnp.bfloat16)
    kept_rounds = []
    for round_index in range(round_total):
        if round_index > 0:
            incoming = passed_along(outgoing, "section", 1)
        else:
            incoming = jnp.zeros((row_count, model_width), jnp.bfloat16)
        micro_index = round_index - section_index
        is_valid = (micro_index >= 0) & (micro_index < micro_count)
        micro_slot = jnp.clip(micro_index, 0, micro_count - 1)
        layer_input_rows = jnp.where(
            section_index == 0,
            lax.dynamic_index_in_dim(own_inputs, micro_slot, 0, keepdims=False),
            incoming,
        )
        allowed, cos_table, sine_table = layout_for(micro_slot)
        layer_out, kept_values = forward_layer(
            layer_input_rows, matrices, allowed, cos_table, sine_table
        )
        kept_rounds.append(kept_values)
        finished = is_valid & (section_index == sections - 1)
        results = jnp.where(
            finished, lax.dynamic_update_index_in_dim(results, layer_out, micro_slot, 0), results
        )
        outgoing = layer_out.astype(jnp.bfloat16)
    stacked = jax.tree.map(lambda *members: jnp.stack(members), *kept_rounds)
    matrices_back = unpack(
        (
            lax.all_gather(shards[0], "dp", axis=0, tiled=True),
            lax.all_gather(shards[1], "dp", axis=0, tiled=True),
            lax.all_gather(shards[2], "dp", axis=0, tiled=True),
            lax.all_gather(shards[3], "dp", axis=0, tiled=True),
            lax.all_gather(shards[4], "dp", axis=0, tiled=True),
            lax.all_gather(shards[5], "dp", axis=0, tiled=True),
            lax.all_gather(shards[6], "dp", axis=0, tiled=True),
            lax.all_gather(shards[7], "dp", axis=0, tiled=True),
        ),
        model_width,
    )
    cotangent = boundary[sections - 1]
    totals = tuple(
        (jnp.zeros((dp_count, shard_piece.shape[1]), jnp.float32) for shard_piece in shards)
    )
    shares = tuple((jnp.zeros(shard_piece.shape, jnp.float32) for shard_piece in shards))
    back_outgoing = jnp.zeros((row_count, model_width), jnp.bfloat16)
    for round_index in range(round_total):
        if round_index > 0:
            arriving = passed_along(back_outgoing, "section", -1)
        else:
            arriving = jnp.zeros((row_count, model_width), jnp.bfloat16)
        micro_index = micro_count - 1 - round_index + (sections - 1 - section_index)
        is_valid = (micro_index >= 0) & (micro_index < micro_count)
        micro_slot = jnp.clip(micro_index, 0, micro_count - 1)
        kept_slot = jnp.clip(micro_index + section_index, 0, round_total - 1)
        kept_values = jax.tree.map(
            lambda member: lax.dynamic_index_in_dim(member, kept_slot, 0, keepdims=False), stacked
        )
        live_now = lax.dynamic_index_in_dim(live_rows, micro_slot, 0, keepdims=False)
        own_grad = (
            lax.dynamic_index_in_dim(cotangent, micro_slot, 0, keepdims=False).astype(jnp.float32)
            * live_now[:, None]
        )
        grad_output = jnp.where(
            section_index == sections - 1, own_grad, arriving.astype(jnp.float32)
        )
        grad_output = grad_output * is_valid.astype(jnp.float32)
        allowed, cos_table, sine_table = layout_for(micro_slot)
        grad_input, grad_terms = backward_layer(
            kept_values, matrices_back, allowed, cos_table, sine_table, grad_output, dp_count
        )
        totals = tuple(
            (left_term + right_term for left_term, right_term in zip(totals, grad_terms))
        )
        results = jnp.where(
            is_valid & (section_index == 0),
            lax.dynamic_update_index_in_dim(results, grad_input, micro_slot, 0),
            results,
        )
        back_outgoing = grad_input.astype(jnp.bfloat16)
    shares = add_sources(
        jax.tree.map(
            lambda part, own: part.astype(own.dtype),
            lax.all_to_all(as_sent(totals), "dp", split_axis=0, concat_axis=0, tiled=True),
            totals,
        )
    )
    return (
        results[None],
        shares[0],
        shares[1],
        shares[2],
        shares[3],
        shares[4],
        shares[5],
        shares[6],
        shares[7],
    )


def solution(mesh):
    placed = (
        P("section", None, "dp", None),
        P(None, "dp", None),
        P("section", "dp"),
        P("section", "dp"),
        P("section", "dp"),
        P("section", "dp"),
        P("section", "dp"),
        P("section", "dp"),
        P("section", "dp"),
        P("section", "dp"),
    )
    return jax.shard_map(
        on_device,
        mesh=mesh,
        in_specs=placed,
        out_specs=(
            P("section", None, "dp", None),
            P("section", "dp"),
            P("section", "dp"),
            P("section", "dp"),
            P("section", "dp"),
            P("section", "dp"),
            P("section", "dp"),
            P("section", "dp"),
            P("section", "dp"),
        ),
        check_vma=False,
    )
```

profile of v0, /device:TPU:0, one launch (start us, length us, event | category | flops | bytes accessed | tf_op | source)
XLA Modules:
  0.0 1352.2 jit_solution(14692853776197630326)
XLA Ops:
  12.2 28.8 %all-gather.1 = bf16[16,1,19200]{2,1,0:T(2,128)(2,1)S(1)} all-gather(bf16[1,1,19200]{2,1,0:T(2,128)(2,1)S(1)} %bitcast.837), channel_id=1, replica_groups=mesh['section'=2,'dp'=16] {'dp'}, dimensions={0}, use_global_device_ids=true | all-gather | bytes 652800 | tf_op jit(solution)/shard_map/all_gather | solution.py:316
  45.7 18.5 %all-gather = bf16[16,1,120]{2,1,0:T(2,128)(2,1)S(1)} all-gather(bf16[1,1,120]{2,1,0:T(2,128)(2,1)S(1)} %bitcast.841), channel_id=1, replica_groups=mesh['section'=2,'dp'=16] {'dp'}, dimensions={0}, use_global_device_ids=true | all-gather | bytes 4080 | tf_op jit(solution)/shard_map/all_gather | solution.py:318
  64.3 26.1 %all-gather.2 = bf16[16,1,19200]{2,1,0:T(2,128)(2,1)} all-gather(bf16[1,1,19200]{2,1,0:T(2,128)(2,1)S(1)} %bitcast.838), channel_id=1, replica_groups=mesh['section'=2,'dp'=16] {'dp'}, dimensions={0}, use_global_device_ids=true | all-gather | bytes 652800 | tf_op jit(solution)/shard_map/all_gather | solution.py:315
  102.4 28.5 %reduce.11 = bf16[16,57600]{1,0:T(8,128)(2,1)} reduce(bf16[16,1,57600]{2,1,0:T(2,128)(2,1)} %all-gather.14.cloned.1.call-done, bf16[]{:T(256)} %constant.374), dimensions={1}, to_apply=%all-gather.3.reduce_sub_computation | reduce | bytes 3686402 | tf_op jit(solution)/shard_map/all_gather | solution.py:314
  137.7 28.3 %reduce.12 = bf16[16,57600]{1,0:T(8,128)(2,1)} reduce(bf16[16,1,57600]{2,1,0:T(2,128)(2,1)} %all-gather.16.cloned.1.call-done, bf16[]{:T(256)} %constant.374), dimensions={1}, to_apply=%all-gather.4.reduce_sub_computation | reduce | bytes 3686402 | tf_op jit(solution)/shard_map/all_gather | solution.py:317
  172.6 7.0 while.84
  181.5 20.3 %all-gather.18.cloned.1.call-done = bf16[16,1,153600]{2,1,0:T(2,128)(2,1)} async-done(((bf16[1,1,153600]{2,1,0:T(2,128)(2,1)}), bf16[16,1,153600]{2,1,0:T(2,128)(2,1)}) %all-gather.18.cloned.1.call-update) | async-done | bytes 4915216 | tf_op jit(solution)/shard_map/all_gather | solution.py:319
  201.8 75.7 %reduce.14 = bf16[16,153600]{1,0:T(8,128)(2,1)} reduce(bf16[16,1,153600]{2,1,0:T(2,128)(2,1)} %all-gather.18.cloned.1.call-done, bf16[]{:T(256)} %constant.374), dimensions={1}, to_apply=%all-gather.5.reduce_sub_computation | reduce | bytes 9830402 | tf_op jit(solution)/shard_map/all_gather | solution.py:319
  277.5 10.5 reshape.1173
  288.0 75.9 %reduce.15 = bf16[16,153600]{1,0:T(8,128)(2,1)} reduce(bf16[16,1,153600]{2,1,0:T(2,128)(2,1)} %all-gather.20.cloned.1.call-done, bf16[]{:T(256)} %constant.374), dimensions={1}, to_apply=%all-gather.6.reduce_sub_computation | reduce | bytes 9830402 | tf_op jit(solution)/shard_map/all_gather | solution.py:320
  363.8 10.5 reshape.1174
  374.4 75.7 %reduce.16 = bf16[16,153600]{1,0:T(8,128)(2,1)} reduce(bf16[16,1,153600]{2,1,0:T(2,128)(2,1)} %all-gather.22.cloned.1.call-done, bf16[]{:T(256)} %constant.374), dimensions={1}, to_apply=%all-gather.7.reduce_sub_computation | reduce | bytes 9830402 | tf_op jit(solution)/shard_map/all_gather | solution.py:321
  450.1 9.6 reshape.1175
  484.7 16.5 %while.85 = (s32[]{:T(128)}, bf16[5,128,3,64]{1,3,2,0:T(8,128)(2,1)}, f32[5,3,128]{2,1,0:T(4,128)}, bf16[5,128,64]{1,2,0:T(8,128)(2,1)}, bf16[5,128,64]{1,2,0:T(...) while((s32[]{:T(128)}, bf16[5,128,3,64]{1,3,2,0:T(8,128)(2,1)}, ...), condition=%wide.region_16.17_spmd.clone, body=%wide.region_13.16_spmd.clone.sunk | while | flops 13024898 | bytes 818273 | solution.py:125
  529.3 20.2 %while.86 = (s32[]{:T(128)}, bf16[5,128,3,64]{1,3,2,0:T(8,128)(2,1)}, f32[5,3,128]{2,1,0:T(4,128)}, bf16[5,128,64]{1,2,0:T(8,128)(2,1)}, bf16[5,128,64]{1,2,0:T(...) while((s32[]{:T(128)}, bf16[5,128,3,64]{1,3,2,0:T(8,128)(2,1)}, ...), condition=%wide.region_22.23_spmd.clone, body=%wide.region_19.22_spmd.clone.sunk | while | flops 13024898 | bytes 818273 | solution.py:125
  566.0 28.6 %while.87 = (s32[]{:T(128)}, f32[5,128,3,64]{1,3,2,0:T(8,128)S(1)}, f32[5,128,64]{1,2,0:T(8,128)S(1)}, bf16[5,128,64]{1,2,0:T(8,128)(2,1)S(1)}, bf16[5,128,64]{1...) while((s32[]{:T(128)}, f32[5,128,3,64]{1,3,2,0:T(8,128)S(1)}, ...), condition=%wide.region_27.28_spmd.clone, body=%wide.region_25.27_spmd.clone.sunk | while | flops 31981184 | bytes 1930361 | solution.py:242
  627.0 31.9 %while.88 = (s32[]{:T(128)}, f32[5,128,3,64]{1,3,2,0:T(8,128)}, f32[5,128,64]{1,2,0:T(8,128)S(1)}, bf16[5,128,64]{1,2,0:T(8,128)(2,1)S(1)}, bf16[5,128,64]{1,2,0...) while((s32[]{:T(128)}, f32[5,128,3,64]{1,3,2,0:T(8,128)}, ...), condition=%wide.region_32.33_spmd.clone, body=%wide.region_30.32_spmd.clone.sunk | while | flops 31981184 | bytes 1930361 | solution.py:242
  683.2 28.8 %while.89 = (s32[]{:T(128)}, f32[5,128,3,64]{1,3,2,0:T(8,128)S(1)}, f32[5,128,64]{1,2,0:T(8,128)S(1)}, bf16[5,128,64]{1,2,0:T(8,128)(2,1)S(1)}, bf16[5,128,64]{1...) while((s32[]{:T(128)}, f32[5,128,3,64]{1,3,2,0:T(8,128)S(1)}, ...), condition=%wide.region_37.38_spmd.clone, body=%wide.region_35.37_spmd.clone.sunk | while | flops 31981184 | bytes 1930361 | solution.py:242
  772.6 27.7 %reduce.23 = bf16[16,57600]{1,0:T(8,128)(2,1)S(1)} reduce(bf16[16,1,57600]{2,1,0:T(2,128)(2,1)} %convert_element_type.718, bf16[]{:T(256)} %broadcast.589), dimensions={1}, to_apply=%convert_element_type.718.reduce_sub_computation | reduce | bytes 3686402 | tf_op jit(solution)/shard_map/convert_element_type | solution.py:20
  812.4 6.8 convert_element_type.721
  819.3 29.0 %reduce.26 = bf16[16,57600]{1,0:T(8,128)(2,1)} reduce(bf16[16,1,57600]{2,1,0:T(2,128)(2,1)} %convert_element_type.721, bf16[]{:T(256)} %broadcast.589), dimensions={1}, to_apply=%convert_element_type.721.reduce_sub_computation | reduce | bytes 3686402 | tf_op jit(solution)/shard_map/convert_element_type | solution.py:20
  851.0 6.4 all-to-all-start.3
  864.1 7.9 add_convert_fusion.2
  872.0 8.5 convert_element_type.722
  880.5 76.4 %reduce.27 = bf16[16,153600]{1,0:T(8,128)(2,1)} reduce(bf16[16,1,153600]{2,1,0:T(2,128)(2,1)} %convert_element_type.722, bf16[]{:T(256)} %broadcast.589), dimensions={1}, to_apply=%convert_element_type.722.reduce_sub_computation | reduce | bytes 9830402 | tf_op jit(solution)/shard_map/convert_element_type | solution.py:20
  957.0 7.6 reshape.1269
  964.5 6.7 all-to-all-start.5
  978.0 8.0 add_convert_fusion.1
  985.9 8.5 convert_element_type.723
  994.5 76.5 %reduce.28 = bf16[16,153600]{1,0:T(8,128)(2,1)} reduce(bf16[16,1,153600]{2,1,0:T(2,128)(2,1)} %convert_element_type.723, bf16[]{:T(256)} %broadcast.589), dimensions={1}, to_apply=%convert_element_type.723.reduce_sub_computation | reduce | bytes 9830402 | tf_op jit(solution)/shard_map/convert_element_type | solution.py:20
  1070.9 7.5 reshape.1271
  1078.5 6.5 all-to-all-start.6
  1092.8 7.7 add_convert_fusion
  1100.5 7.9 copy.144
  1108.4 13.5 convert_element_type.724
  1121.9 76.4 %reduce.29 = bf16[16,153600]{1,0:T(8,128)(2,1)} reduce(bf16[16,1,153600]{2,1,0:T(2,128)(2,1)} %convert_element_type.724, bf16[]{:T(256)} %broadcast.589), dimensions={1}, to_apply=%convert_element_type.724.reduce_sub_computation | reduce | bytes 9830402 | tf_op jit(solution)/shard_map/convert_element_type | solution.py:20
  1198.3 7.5 reshape.1273
  1205.9 6.5 all-to-all-start.7
  1233.0 12.0 reshape.1262
  1245.0 6.4 convert_reduce_fusion.4
  1252.2 12.2 reshape.1268
  1264.4 6.4 convert_reduce_fusion.3
  1271.6 12.7 reshape.1270
  1284.4 12.7 reshape.1272
  1297.1 12.4 convert_reduce_fusion.2
  1309.4 10.9 convert_reduce_fusion.1
  1320.3 12.7 reshape.1274
  1333.0 12.2 convert_reduce_fusion
  (773 shorter events, 411.2 us)
Async XLA Ops:
  7.2 95.2 %all-gather.14.cloned.1.call-start = ((), (), s32[]{:S(2)}) async-start(), calls=%async_computation.8 | async-start | bytes 3916800 | tf_op jit(solution)/shard_map/all_gather | solution.py:314
  7.9 129.7 %all-gather.16.cloned.1.call-start = ((), (), s32[]{:S(2)}) async-start(), calls=%async_computation.9 | async-start | bytes 3916800 | tf_op jit(solution)/shard_map/all_gather | solution.py:317
  8.7 193.1 %all-gather.18.cloned.1.call-start = ((), (), s32[]{:S(2)}) async-start(), calls=%async_computation.10 | async-start | bytes 10444800 | tf_op jit(solution)/shard_map/all_gather | solution.py:319
  9.4 278.6 %all-gather.20.cloned.1.call-start = ((), (), s32[]{:S(2)}) async-start(), calls=%async_computation.11 | async-start | bytes 10444800 | tf_op jit(solution)/shard_map/all_gather | solution.py:320
  10.0 364.4 %all-gather.22.cloned.1.call-start = ((), (), s32[]{:S(2)}) async-start(), calls=%async_computation.12 | async-start | bytes 10444800 | tf_op jit(solution)/shard_map/all_gather | solution.py:321
  10.6 35.1 %copy-start.47 = (bf16[5,128,3,64]{1,3,2,0:T(8,128)(2,1)}, bf16[5,128,3,64]{1,3,2,0:T(8,128)(2,1)S(1)}, u32[]{:S(2)}) copy-start(bf16[5,128,3,64]{1,3,2,0:T(8,128)(2,1)S(1)} %fusion.320) | copy-start | bytes 737284
  12.2 33.5 %copy-start.149 = (bf16[1,120]{1,0:T(2,128)(2,1)S(1)}, bf16[1,120]{1,0:T(2,128)(2,1)}, u32[]{:S(2)}) copy-start(bf16[1,120]{1,0:T(2,128)(2,1)} %param.28) | copy-start | bytes 724
  12.2 52.1 %copy-start.118 = (bf16[1,19200]{1,0:T(2,128)(2,1)S(1)}, bf16[1,19200]{1,0:T(2,128)(2,1)}, u32[]{:S(2)}) copy-start(bf16[1,19200]{1,0:T(2,128)(2,1)} %param.25) | copy-start | bytes 115204
  45.7 55.4 %copy-start.32 = (bf16[960,320]{1,0:T(8,128)(2,1)}, bf16[960,320]{1,0:T(8,128)(2,1)S(1)}, u32[]{:S(2)}) copy-start(bf16[960,320]{1,0:T(8,128)(2,1)S(1)} %reshape.1165) | copy-start | bytes 1843204
  99.9 72.5 %copy-start.104 = (f32[128,64]{0,1:T(8,128)}, f32[128,64]{0,1:T(8,128)S(1)}, u32[]{:S(2)}) copy-start(f32[128,64]{0,1:T(8,128)S(1)} %pad_maximum_fusion.3) | copy-start | bytes 98308
  99.9 72.5 %copy-start.102 = (f32[128,64]{0,1:T(8,128)}, f32[128,64]{0,1:T(8,128)S(1)}, u32[]{:S(2)}) copy-start(f32[128,64]{0,1:T(8,128)S(1)} %pad_maximum_fusion.2) | copy-start | bytes 98308
  100.6 69.4 %copy-start.127 = (f32[128]{0:T(128)}, f32[128]{0:T(128)S(1)}, u32[]{:S(2)}) copy-start(f32[128]{0:T(128)S(1)} %add_rsqrt_fusion.5) | copy-start | bytes 1540
  179.7 97.8 %copy-start.94 = (bf16[5,128,64]{1,2,0:T(8,128)(2,1)}, bf16[5,128,64]{1,2,0:T(8,128)(2,1)S(1)}, u32[]{:S(2)}) copy-start(bf16[5,128,64]{1,2,0:T(8,128)(2,1)S(1)} %get-tuple-element.1174) | copy-start | bytes 245764
  179.7 97.8 %copy-start.121 = (f32[5,3,128]{2,1,0:T(4,128)}, f32[5,3,128]{2,1,0:T(4,128)S(1)}, u32[]{:S(2)}) copy-start(f32[5,3,128]{2,1,0:T(4,128)S(1)} %get-tuple-element.1124) | copy-start | bytes 23044
  181.2 284.4 %copy-start.30 = (f32[128,960]{0,1:T(8,128)}, f32[128,960]{0,1:T(8,128)S(1)}, u32[]{:S(2)}) copy-start(f32[128,960]{0,1:T(8,128)S(1)} %get-tuple-element.617) | copy-start | bytes 1474564
  181.2 96.2 %copy-start.140 = (f32[128]{0:T(128)}, f32[128]{0:T(128)S(1)}, u32[]{:S(2)}) copy-start(f32[128]{0:T(128)S(1)} %add_rsqrt_fusion.4) | copy-start | bytes 1540
  181.5 281.7 %copy-start.36 = (bf16[128,960]{0,1:T(8,128)(2,1)}, bf16[128,960]{0,1:T(8,128)(2,1)S(1)}, u32[]{:S(2)}) copy-start(bf16[128,960]{0,1:T(8,128)(2,1)S(1)} %multiply_convert_fusion.15) | copy-start | bytes 737284
  469.1 12.1 copy-start.58
  469.1 9.6 collective-permute-start
  474.6 45.2 %copy-start.83 = (bf16[5,128,64]{1,2,0:T(8,128)(2,1)}, bf16[5,128,64]{1,2,0:T(8,128)(2,1)S(1)}, u32[]{:S(2)}) copy-start(bf16[5,128,64]{1,2,0:T(8,128)(2,1)S(1)} %fusion.322) | copy-start | bytes 245764
  484.7 22.7 %slice-start = ((s8[4915200]{0:T(1024)(128)(4,1)}), s8[720896]{0:T(1024)(128)(4,1)S(1)}, s32[]{:S(2)}) async-start(s8[4915200]{0:T(1024)(128)(4,1)} %bitcast.771), calls=%async_computation.13 | async-start | bytes 1441792
  509.6 9.6 copy-start.137
  509.6 10.2 copy-start.119
  513.1 13.4 copy-start.59
  513.1 10.8 collective-permute-start.1
  529.3 26.5 %slice-start.2 = ((s8[4915200]{0:T(1024)(128)(4,1)}), s8[720896]{0:T(1024)(128)(4,1)S(1)}, s32[]{:S(2)}) async-start(s8[4915200]{0:T(1024)(128)(4,1)} %bitcast.773), calls=%async_computation.15 | async-start | bytes 1441792
  551.5 12.0 copy-start.20
  600.7 20.6 %slice-start.4 = ((s8[4915200]{0:T(1024)(128)(4,1)}), s8[720896]{0:T(1024)(128)(4,1)S(1)}, s32[]{:S(2)}) async-start(s8[4915200]{0:T(1024)(128)(4,1)} %bitcast.775), calls=%async_computation.17 | async-start | bytes 1441792
  601.6 9.8 collective-permute-start.2
  611.4 9.9 slice-start.5
  624.7 39.0 %copy-start.27 = (f32[128,960]{0,1:T(8,128)}, f32[128,960]{0,1:T(8,128)S(1)}, u32[]{:S(2)}) copy-start(f32[128,960]{0,1:T(8,128)S(1)} %multiply_add_fusion.1) | copy-start | bytes 1474564
  627.0 33.5 %copy-start.108 = (f32[128,64]{0,1:T(8,128)S(1)}, f32[128,64]{0,1:T(8,128)}, u32[]{:S(2)}) copy-start(f32[128,64]{0,1:T(8,128)} %pad_maximum_fusion.5) | copy-start | bytes 98308
  664.6 8.3 collective-permute-start.3
  666.9 11.4 slice-start.10
  666.9 12.9 slice-start.6
  683.2 28.8 %copy-start.33 = (bf16[960,320]{1,0:T(8,128)(2,1)S(1)}, bf16[960,320]{1,0:T(8,128)(2,1)}, u32[]{:S(2)}) copy-start(bf16[960,320]{1,0:T(8,128)(2,1)} %copy-done.32) | copy-start | bytes 1843204
  683.2 29.9 %copy-start.105 = (f32[128,64]{0,1:T(8,128)S(1)}, f32[128,64]{0,1:T(8,128)}, u32[]{:S(2)}) copy-start(f32[128,64]{0,1:T(8,128)} %copy-done.104) | copy-start | bytes 98308
  720.6 17.5 %all-to-all-start.4 = ((bf16[16,1,120]{2,1,0:T(2,128)(2,1)}), bf16[16,1,120]{2,1,0:T(2,128)(2,1)S(1)}, u32[]{:S(2)}, u32[]{:S(2)}) async-start(bf16[16,1,120]{2,1,0:T(2,128)(2,1)} %fusion.264), calls=%async_computation.4 | async-start | bytes 16384 | tf_op jit(solution)/shard_map/all_to_all | solution.py:409
  730.8 13.6 %copy-start.42 = (f32[5,128,3,64]{1,3,2,0:T(8,128)S(1)}, f32[5,128,3,64]{1,3,2,0:T(8,128)}, u32[]{:S(2)}) copy-start(f32[5,128,3,64]{1,3,2,0:T(8,128)} %copy-done.41) | copy-start | bytes 1474564
  730.8 13.6 %copy-start.98 = (f32[128,64]{0,1:T(8,128)S(1)}, f32[128,64]{0,1:T(8,128)}, u32[]{:S(2)}) copy-start(f32[128,64]{0,1:T(8,128)} %copy-done.96) | copy-start | bytes 98308
  738.1 22.3 %all-to-all-start.1 = ((bf16[16,2,9600]{2,1,0:T(2,128)(2,1)}), bf16[16,2,9600]{2,1,0:T(2,128)(2,1)}, u32[]{:S(2)}, u32[]{:S(2)}) async-start(bf16[16,2,9600]{2,1,0:T(2,128)(2,1)} %reshape.1263), calls=%async_computation.1 | async-start | bytes 1228800 | tf_op jit(solution)/shard_map/all_to_all | solution.py:409
  760.4 41.6 %all-to-all-start.2 = ((bf16[16,2,9600]{2,1,0:T(2,128)(2,1)}), bf16[16,2,9600]{2,1,0:T(2,128)(2,1)}, u32[]{:S(2)}, u32[]{:S(2)}) async-start(bf16[16,2,9600]{2,1,0:T(2,128)(2,1)} %reshape.1265), calls=%async_computation.2 | async-start | bytes 1228800 | tf_op jit(solution)/shard_map/all_to_all | solution.py:409
  801.9 49.0 %all-to-all-start = ((bf16[16,2,28800]{2,1,0:T(2,128)(2,1)}), bf16[16,2,28800]{2,1,0:T(2,128)(2,1)}, u32[]{:S(2)}, u32[]{:S(2)}) async-start(bf16[16,2,28800]{2,1,0:T(2,128)(2,1)} %reshape.1261), calls=%async_computation | async-start | bytes 3686400 | tf_op jit(solution)/shard_map/all_to_all | solution.py:409
  851.0 113.6 %all-to-all-start.3 = ((bf16[16,2,28800]{2,1,0:T(2,128)(2,1)}), bf16[16,2,28800]{2,1,0:T(2,128)(2,1)}, u32[]{:S(2)}, u32[]{:S(2)}) async-start(bf16[16,2,28800]{2,1,0:T(2,128)(2,1)} %reshape.1267), calls=%async_computation.3 | async-start | bytes 3686400 | tf_op jit(solution)/shard_map/all_to_all | solution.py:409
  964.5 114.0 %all-to-all-start.5 = ((bf16[16,2,76800]{2,1,0:T(2,128)(2,1)}), bf16[16,2,76800]{2,1,0:T(2,128)(2,1)}, u32[]{:S(2)}, u32[]{:S(2)}) async-start(bf16[16,2,76800]{2,1,0:T(2,128)(2,1)} %reshape.1269), calls=%async_computation.5 | async-start | bytes 9830400 | tf_op jit(solution)/shard_map/all_to_all | solution.py:409
  1078.5 127.4 %all-to-all-start.6 = ((bf16[16,2,76800]{2,1,0:T(2,128)(2,1)}), bf16[16,2,76800]{2,1,0:T(2,128)(2,1)}, u32[]{:S(2)}, u32[]{:S(2)}) async-start(bf16[16,2,76800]{2,1,0:T(2,128)(2,1)} %reshape.1271), calls=%async_computation.6 | async-start | bytes 9830400 | tf_op jit(solution)/shard_map/all_to_all | solution.py:409
  1205.9 114.4 %all-to-all-start.7 = ((bf16[16,2,76800]{2,1,0:T(2,128)(2,1)}), bf16[16,2,76800]{2,1,0:T(2,128)(2,1)}, u32[]{:S(2)}, u32[]{:S(2)}) async-start(bf16[16,2,76800]{2,1,0:T(2,128)(2,1)} %reshape.1273), calls=%async_computation.7 | async-start | bytes 9830400 | tf_op jit(solution)/shard_map/all_to_all | solution.py:409
  1297.1 12.4 copy-start.5
  (137 other events, 490.6 us)
Sparse Core Ops, SparseCore 0:
  10.3 54.0 all-gather.13
  66.7 49.7 all-gather.15
  118.7 83.0 all-gather.17
  203.9 82.0 all-gather.19
  288.1 82.0 all-gather.21
where the time goes:
time: 1370 us; the launch traced here: 1350 us
  other arithmetic  671 us (49%)
  matrix products  251 us (18%)
  local copies, waits for them, and re-layouts  235 us (17%)
  blocking collectives  73.4 us (5%)
  starting transfers between devices  60.9 us (4%)
  waiting for transfers between devices  42.6 us (3%)
  between operations  16.8 us (1%)
    convert_element_type x8, other arithmetic, as_sent(): a.astype(jnp.bfloat16)  296 us
    unnamed x352, local copies, waits for them, and re-layouts  113 us
    all_gather x1, other arithmetic, on_device(): lax.all_gather(shards[6], 'dp', axis=0, tiled=True)  75.9 us
    all_gather x1, other arithmetic, on_device(): lax.all_gather(shards[7], 'dp', axis=0, tiled=True)  75.7 us
    all_gather x1, other arithmetic, on_device(): lax.all_gather(shards[5], 'dp', axis=0, tiled=True)  75.7 us
    convert_element_type x11, local copies, waits for them, and re-layouts, as_sent(): a.astype(jnp.bfloat16)  56.7 us
    reduce_sum x8, other arithmetic, add_sources(): jnp.sum(member, axis=0, keepdims=True)  51.4 us
    all_to_all x8, starting transfers between devices, on_device(): lax.all_to_all(as_sent(totals), 'dp', split_axis=0, concat_axis=0, tiled=...  47.3 us
  transfers between devices with their start and end apart: 17, of which 6 were waited for; matrix products, arithmetic and copies ran while one was open for 61% of the time, Pallas kernels for 0%

commit v1 on v0

--- a/solution.py
+++ b/solution.py
@@ -1,6 +1,10 @@
+import functools
+
 import jax
 import jax.numpy as jnp
 from jax import lax
+from jax.experimental import pallas as pl
+from jax.experimental.pallas import tpu as pltpu
 from jax.sharding import PartitionSpec as P
 
 HEAD = 64
@@ -423,6 +427,695 @@
     )
 
 
+def ring_place(chips):
+    depth = chips // 2
+
+    def place_of(chip):
+        side = chip % 2
+        level = chip // 2
+        return level * (1 - side) + (chips - 1 - level) * side
+
+    def chip_at(place):
+        side = place // depth
+        level = place * (1 - side) + (chips - 1 - place) * side
+        return level * 2 + side
+
+    return place_of, chip_at
+
+
+def ring_setup(chips):
+    place_of, chip_at = ring_place(chips)
+    member = lax.axis_index("dp")
+    core = member % 2
+    place = place_of(member // 2)
+    turn = 1 - 2 * core
+
+    def at(offset, on_core):
+        return chip_at((place + offset + 2 * chips) % chips) * 2 + on_core
+
+    following = at(turn, core)
+    preceding = at(-turn, core)
+    sibling = member + turn
+    barrier = pltpu.get_barrier_semaphore()
+    for other in (following, preceding, sibling):
+        pl.semaphore_signal(
+            barrier, inc=1, device_id={"dp": other}, device_id_type=pl.DeviceIdType.MESH
+        )
+    pl.semaphore_wait(barrier, 3)
+    return member, core, turn, at, following, sibling
+
+
+def gather_kernel(chips, heights, *refs):
+    count = len(heights)
+    pieces = refs[:count]
+    wholes = refs[count : 2 * count]
+    keep_sem, ring_send, ring_recv, side_send, side_recv = refs[2 * count :]
+    member, core, turn, at, following, sibling = ring_setup(chips)
+
+    def rows(index, owner):
+        height = heights[index]
+        return wholes[index].at[pl.ds(pl.multiple_of(owner * height, 16), height), :]
+
+    def ring_copy(index, source, owner, step):
+        return pltpu.make_async_remote_copy(
+            src_ref=source,
+            dst_ref=rows(index, owner),
+            send_sem=ring_send.at[step, index],
+            recv_sem=ring_recv.at[step, index],
+            device_id={"dp": following},
+            device_id_type=pl.DeviceIdType.MESH,
+        )
+
+    def side_copy(index, source, owner, step):
+        return pltpu.make_async_remote_copy(
+            src_ref=source,
+            dst_ref=rows(index, owner),
+            send_sem=side_send.at[step, index],
+            recv_sem=side_recv.at[step, index],
+            device_id={"dp": sibling},
+            device_id_type=pl.DeviceIdType.MESH,
+        )
+
+    for index in range(count):
+        ring_copy(index, pieces[index], member, 0).start()
+    for index in range(count):
+        side_copy(index, pieces[index], member, 0).start()
+        pltpu.make_async_copy(pieces[index], rows(index, member), keep_sem.at[index]).start()
+    for step in range(1, chips):
+        owner = at(-turn * step, core)
+        for index in range(count):
+            ring_copy(index, rows(index, owner), owner, step - 1).wait_recv()
+            if step < chips - 1:
+                ring_copy(index, rows(index, owner), owner, step).start()
+            side_copy(index, rows(index, owner), owner, step).start()
+    for index in range(count):
+        pltpu.make_async_copy(pieces[index], rows(index, member), keep_sem.at[index]).wait()
+    for step in range(chips):
+        owner = at(-turn * step, core)
+        theirs = at(turn * step, 1 - core)
+        for index in range(count):
+            if step < chips - 1:
+                ring_copy(index, rows(index, owner), owner, step).wait_send()
+            side_copy(index, rows(index, owner), owner, step).wait_send()
+            side_copy(index, rows(index, theirs), theirs, step).wait_recv()
+
+
+def gather_all(pieces, members):
+    chips = members // 2
+    heights = tuple(piece.shape[0] for piece in pieces)
+    count = len(pieces)
+    return pl.pallas_call(
+        functools.partial(gather_kernel, chips, heights),
+        out_shape=tuple(
+            jax.ShapeDtypeStruct((members * piece.shape[0], piece.shape[1]), piece.dtype)
+            for piece in pieces
+        ),
+        in_specs=[pl.BlockSpec(memory_space=pl.ANY)] * count,
+        out_specs=tuple([pl.BlockSpec(memory_space=pl.ANY)] * count),
+        scratch_shapes=[pltpu.SemaphoreType.DMA((count,))]
+        + [pltpu.SemaphoreType.DMA((chips, count))] * 4,
+        compiler_params=pltpu.CompilerParams(collective_id=0, has_side_effects=True),
+        name="gather_ring",
+    )(*pieces)
+
+
+def scatter_kernel(chips, heights, *refs):
+    count = len(heights)
+    terms = refs[:count]
+    totals = refs[count : 2 * count]
+    owns = refs[2 * count : 3 * count]
+    sides = refs[3 * count : 4 * count]
+    rings = refs[4 * count : 5 * count]
+    load_sem, ring_send, ring_recv, side_send, side_recv = refs[5 * count :]
+    member, core, turn, at, following, sibling = ring_setup(chips)
+
+    def rows(index, owner):
+        height = heights[index]
+        return terms[index].at[pl.ds(pl.multiple_of(owner * height, 16), height), :]
+
+    def load(index, step):
+        owner = at(-turn * (step + 1), core)
+        return pltpu.make_async_copy(
+            rows(index, owner), owns[index].at[step], load_sem.at[step, index]
+        )
+
+    def side_copy(index, step):
+        owner = at(turn * (step + 1), 1 - core)
+        return pltpu.make_async_remote_copy(
+            src_ref=rows(index, owner),
+            dst_ref=sides[index].at[step],
+            send_sem=side_send.at[step, index],
+            recv_sem=side_recv.at[step, index],
+            device_id={"dp": sibling},
+            device_id_type=pl.DeviceIdType.MESH,
+        )
+
+    def ring_copy(index, step):
+        return pltpu.make_async_remote_copy(
+            src_ref=owns[index].at[step],
+            dst_ref=rings[index].at[step],
+            send_sem=ring_send.at[step, index],
+            recv_sem=ring_recv.at[step, index],
+            device_id={"dp": following},
+            device_id_type=pl.DeviceIdType.MESH,
+        )
+
+    for step in range(chips):
+        for index in range(count):
+            side_copy(index, step).start()
+            load(index, step).start()
+    for step in range(chips):
+        for index in range(count):
+            load(index, step).wait()
+            side_copy(index, step).wait_recv()
+            if step > 0:
+                ring_copy(index, step - 1).wait_recv()
+
+            def add(block):
+                part = pl.ds(pl.multiple_of(block * 16, 16), 16)
+                total = owns[index][step, part, :].astype(jnp.float32) + sides[index][
+                    step, part, :
+                ].astype(jnp.float32)
+                if step > 0:
+                    total = total + rings[index][step - 1, part, :].astype(jnp.float32)
+                if step < chips - 1:
+                    owns[index][step, part, :] = total.astype(jnp.bfloat16)
+                else:
+                    totals[index][part, :] = total
+
+            pl.loop(0, heights[index] // 16)(add)
+            if step < chips - 1:
+                ring_copy(index, step).start()
+    for step in range(chips):
+        for index in range(count):
+            side_copy(index, step).wait_send()
+            if step < chips - 1:
+                ring_copy(index, step).wait_send()
+
+
+def scatter_all(terms, members):
+    chips = members // 2
+    heights = tuple(term.shape[0] // members for term in terms)
+    widths = tuple(term.shape[1] for term in terms)
+    count = len(terms)
+    stacks = lambda depth: [
+        pltpu.VMEM((depth, height, width), jnp.bfloat16) for height, width in zip(heights, widths)
+    ]
+    return pl.pallas_call(
+        functools.partial(scatter_kernel, chips, heights),
+        out_shape=tuple(
+            jax.ShapeDtypeStruct((height, width), jnp.float32)
+            for height, width in zip(heights, widths)
+        ),
+        in_specs=[pl.BlockSpec(memory_space=pl.ANY)] * count,
+        out_specs=tuple([pl.BlockSpec(memory_space=pltpu.VMEM)] * count),
+        scratch_shapes=stacks(chips)
+        + stacks(chips)
+        + stacks(chips - 1)
+        + [pltpu.SemaphoreType.DMA((chips, count))] * 5,
+        compiler_params=pltpu.CompilerParams(
+            collective_id=1, has_side_effects=True, vmem_limit_bytes=56 * 2**20
+        ),
+        name="scatter_ring",
+    )(*terms)
+
+
+def dot(left, right):
+    return jnp.dot(left, right, preferred_element_type=jnp.float32)
+
+
+def dot_nt(left, right):
+    return lax.dot_general(
+        left, right, (((1,), (1,)), ((), ())), preferred_element_type=jnp.float32
+    )
+
+
+def dot_tn(left, right):
+    return lax.dot_general(
+        left, right, (((0,), (0,)), ((), ())), preferred_element_type=jnp.float32
+    )
+
+
+def turn_heads(values, tables, sign):
+    width = values.shape[1]
+    cos_table, early_sine, late_sine = tables
+    half = HEAD // 2
+    return values * cos_table[...] + sign * (
+        pltpu.roll(values, width - half, 1) * early_sine[...]
+        + pltpu.roll(values, half, 1) * late_sine[...]
+    )
+
+
+def head_rows(source, micro, rows, first, group):
+    return jnp.concatenate(
+        [
+            source[micro * rows : (micro + 1) * rows, (first + g) * HEAD : (first + g + 1) * HEAD]
+            for g in range(group)
+        ],
+        axis=0,
+    )
+
+
+def forward_kernel(
+    model,
+    layout,
+    stream,
+    gains,
+    bias,
+    cos_table,
+    early_sine,
+    late_sine,
+    spread,
+    w_qkv,
+    w_out,
+    w_gate,
+    w_up,
+    w_down,
+    layer_out,
+    normed,
+    turned,
+    values,
+    mixed_wide,
+    middle,
+    normed_two,
+    gate_pre,
+    up_pre,
+    activation,
+    mixed,
+):
+    heads, kv_heads, micro_count, rows = layout
+    group = heads // kv_heads
+
+    @pl.when(pl.program_id(0) == 0)
+    def _():
+        residual = stream[...]
+        scale = lax.rsqrt(jnp.sum(residual * residual, axis=1, keepdims=True) / model + EPSILON)
+        normed[...] = (residual * scale * gains[0:1, :]).astype(jnp.bfloat16)
+        products = dot(normed[...], w_qkv[...])
+        split = (heads + kv_heads) * HEAD
+        turned[...] = turn_heads(
+            products[:, :split], (cos_table, early_sine, late_sine), 1.0
+        ).astype(jnp.bfloat16)
+        values[...] = products[:, split:].astype(jnp.bfloat16)
+        for micro in range(micro_count):
+            part = slice(micro * rows, (micro + 1) * rows)
+            for kv in range(kv_heads):
+                query = head_rows(turned, micro, rows, kv * group, group)
+                key = turned[part, (heads + kv) * HEAD : (heads + kv + 1) * HEAD]
+                value = values[part, kv * HEAD : (kv + 1) * HEAD]
+                scores = dot_nt(query, key) * HEAD ** (-0.5)
+                scores = scores + jnp.concatenate([bias[micro]] * group, axis=0)
+                exponent = jnp.exp(scores - jnp.max(scores, axis=1, keepdims=True))
+                total = jnp.sum(exponent, axis=1, keepdims=True)
+                probability = (exponent / total).astype(jnp.bfloat16)
+                attended = dot(probability, value).astype(jnp.bfloat16)
+                for g in range(group):
+                    head = kv * group + g
+                    mixed[part, head * HEAD : (head + 1) * HEAD] = attended[
+                        g * rows : (g + 1) * rows, :
+                    ]
+        mixed_wide[...] = dot(mixed[...], spread[...]).astype(jnp.bfloat16)
+        halfway = residual + dot(mixed_wide[...], w_out[...])
+        middle[...] = halfway
+        scale_two = lax.rsqrt(jnp.sum(halfway * halfway, axis=1, keepdims=True) / model + EPSILON)
+        normed_two[...] = (halfway * scale_two * gains[1:2, :]).astype(jnp.bfloat16)
+        layer_out[...] = halfway
+
+    gate = dot(normed_two[...], w_gate[...])
+    up = dot(normed_two[...], w_up[...])
+    gate_pre[...] = gate
+    up_pre[...] = up
+    active = (gate * jax.nn.sigmoid(gate) * up).astype(jnp.bfloat16)
+    activation[...] = active
+    layer_out[...] += dot(active, w_down[...])
+
+
+def full(array):
+    return pl.BlockSpec(array.shape, lambda i: (0,) * len(array.shape))
+
+
+def shape_of(rows, width, dtype):
+    return jax.ShapeDtypeStruct((rows, width), dtype)
+
+
+def tile_width(hidden):
+    for width in (512, 256, 128):
+        if hidden % width == 0:
+            return width
+    return hidden
+
+
+def forward_fast(model, layout, stream, gains, bias, tables, spread, matrices):
+    w_qkv, w_out, w_gate, w_up, w_down = matrices
+    heads, kv_heads, micro_count, rows = layout
+    tokens, wide = stream.shape
+    hidden = w_gate.shape[1]
+    tile = tile_width(hidden)
+    split = (heads + kv_heads) * HEAD
+    low, high = jnp.bfloat16, jnp.float32
+    out_shape = (
+        shape_of(tokens, wide, high),
+        shape_of(tokens, wide, low),
+        shape_of(tokens, split, low),
+        shape_of(tokens, w_qkv.shape[1] - split, low),
+        shape_of(tokens, wide, low),
+        shape_of(tokens, wide, high),
+        shape_of(tokens, wide, low),
+        shape_of(tokens, hidden, high),
+        shape_of(tokens, hidden, high),
+        shape_of(tokens, hidden, low),
+    )
+    columns = lambda height: pl.BlockSpec((height, tile), lambda i: (0, i))
+    ins = (stream, gains, bias, *tables, spread, w_qkv, w_out)
+    return pl.pallas_call(
+        functools.partial(forward_kernel, model, layout),
+        grid=(hidden // tile,),
+        out_shape=out_shape,
+        in_specs=[full(member) for member in ins]
+        + [columns(wide), columns(wide), pl.BlockSpec((tile, wide), lambda i: (i, 0))],
+        out_specs=tuple([full(member) for member in out_shape[:7]] + [columns(tokens)] * 3),
+        scratch_shapes=[pltpu.VMEM((tokens, heads * HEAD), low)],
+        compiler_params=pltpu.CompilerParams(vmem_limit_bytes=56 * 2**20),
+        cost_estimate=pl.CostEstimate(
+            flops=20 * 2**28, bytes_accessed=30 * 2**20, transcendentals=2**20
+        ),
+        name="forward_layer",
+    )(*ins, w_gate, w_up, w_down)
+
+
+def backward_kernel(
+    model,
+    layout,
+    cotangent,
+    stream,
+    gains,
+    bias,
+    cos_table,
+    early_sine,
+    late_sine,
+    spread,
+    turned,
+    values,
+    middle,
+    w_qkv,
+    w_out,
+    gate_pre,
+    up_pre,
+    w_gate,
+    w_up,
+    w_down,
+    grad_input,
+    grad_low,
+    grad_gains,
+    grad_branch,
+    grad_qkv,
+    grad_gate,
+    grad_up,
+    norm_grad,
+    grad_mixed,
+    grad_turned,
+    grad_values,
+):
+    heads, kv_heads, micro_count, rows = layout
+    group = heads // kv_heads
+    step = pl.program_id(0)
+
+    @pl.when(step == 0)
+    def _():
+        grad_low[...] = cotangent[...].astype(jnp.bfloat16)
+        norm_grad[...] = jnp.zeros_like(norm_grad)
+
+    gate = gate_pre[...]
+    grad_act = dot_nt(grad_low[...], w_down[...])
+    sigmoid = jax.nn.sigmoid(gate)
+    grad_gate[...] = (
+        grad_act * up_pre[...] * sigmoid * (1.0 + gate * (1.0 - sigmoid))
+    ).astype(jnp.bfloat16)
+    grad_up[...] = (grad_act * gate * sigmoid).astype(jnp.bfloat16)
+    norm_grad[...] += dot_nt(grad_gate[...], w_gate[...]) + dot_nt(grad_up[...], w_up[...])
+
+    @pl.when(step == pl.num_programs(0) - 1)
+    def _():
+        halfway = middle[...]
+        scale_two = lax.rsqrt(jnp.sum(halfway * halfway, axis=1, keepdims=True) / model + EPSILON)
+        centered = halfway * scale_two
+        gradient = norm_grad[...]
+        grad_gains[1:2, :] = jnp.sum(gradient * centered, axis=0, keepdims=True)
+        scaled = gradient * gains[1:2, :]
+        grad_middle = cotangent[...] + scale_two * (
+            scaled - centered * (jnp.sum(scaled * centered, axis=1, keepdims=True) / model)
+        )
+        grad_input[...] = grad_middle
+        grad_branch[...] = grad_middle.astype(jnp.bfloat16)
+        grad_wide = dot_nt(grad_branch[...], w_out[...]).astype(jnp.bfloat16)
+        grad_mixed[...] = dot_nt(grad_wide, spread[...]).astype(jnp.bfloat16)
+        grad_values[...] = jnp.zeros_like(grad_values)
+        for micro in range(micro_count):
+            part = slice(micro * rows, (micro + 1) * rows)
+            for kv in range(kv_heads):
+                query = head_rows(turned, micro, rows, kv * group, group)
+                key = turned[part, (heads + kv) * HEAD : (heads + kv + 1) * HEAD]
+                value = values[part, kv * HEAD : (kv + 1) * HEAD]
+                grad_head = head_rows(grad_mixed, micro, rows, kv * group, group)
+                scores = dot_nt(query, key) * HEAD ** (-0.5)
+                scores = scores + jnp.concatenate([bias[micro]] * group, axis=0)
+                exponent = jnp.exp(scores - jnp.max(scores, axis=1, keepdims=True))
+                total = jnp.sum(exponent, axis=1, keepdims=True)
+                probability = exponent / total
+                grad_value = dot_tn(probability.astype(jnp.bfloat16), grad_head)
+                grad_prob = dot_nt(grad_head, value)
+                inner = jnp.sum(probability * grad_prob, axis=1, keepdims=True)
+                grad_scores = (probability * (grad_prob - inner)).astype(jnp.bfloat16)
+                grad_query = dot(grad_scores, key) * HEAD ** (-0.5)
+                grad_key = dot_tn(grad_scores, query) * HEAD ** (-0.5)
+                for g in range(group):
+                    head = kv * group + g
+                    grad_turned[part, head * HEAD : (head + 1) * HEAD] = grad_query[
+                        g * rows : (g + 1) * rows, :
+                    ]
+                grad_turned[part, (heads + kv) * HEAD : (heads + kv + 1) * HEAD] = grad_key
+                grad_values[part, kv * HEAD : (kv + 1) * HEAD] = grad_value
+        split = (heads + kv_heads) * HEAD
+        grad_qkv[:, :split] = turn_heads(
+            grad_turned[...], (cos_table, early_sine, late_sine), -1.0
+        ).astype(jnp.bfloat16)
+        grad_qkv[:, split:] = grad_values[...].astype(jnp.bfloat16)
+        first_gradient = dot_nt(grad_qkv[...], w_qkv[...])
+        residual = stream[...]
+        scale = lax.rsqrt(jnp.sum(residual * residual, axis=1, keepdims=True) / model + EPSILON)
+        first_centered = residual * scale
+        grad_gains[0:1, :] = jnp.sum(first_gradient * first_centered, axis=0, keepdims=True)
+        first_scaled = first_gradient * gains[0:1, :]
+        grad_input[...] += scale * (
+            first_scaled
+            - first_centered
+            * (jnp.sum(first_scaled * first_centered, axis=1, keepdims=True) / model)
+        )
+
+
+def backward_fast(model, layout, cotangent, kept, gains, bias, tables, spread, matrices):
+    w_qkv, w_out, w_gate, w_up, w_down = matrices
+    stream, _, turned, values, _, middle, _, gate_pre, up_pre, _ = kept
+    heads, kv_heads, micro_count, rows = layout
+    tokens, wide = stream.shape
+    hidden = w_gate.shape[1]
+    tile = tile_width(hidden)
+    split = (heads + kv_heads) * HEAD
+    low, high = jnp.bfloat16, jnp.float32
+    out_shape = (
+        shape_of(tokens, wide, high),
+        shape_of(tokens, wide, low),
+        shape_of(2, wide, high),
+        shape_of(tokens, wide, low),
+        shape_of(tokens, w_qkv.shape[1], low),
+        shape_of(tokens, hidden, low),
+        shape_of(tokens, hidden, low),
+    )
+    columns = lambda height: pl.BlockSpec((height, tile), lambda i: (0, i))
+    ins = (cotangent, stream, gains, bias, *tables, spread, turned, values, middle, w_qkv, w_out)
+    return pl.pallas_call(
+        functools.partial(backward_kernel, model, layout),
+        grid=(hidden // tile,),
+        out_shape=out_shape,
+        in_specs=[full(member) for member in ins]
+        + [columns(tokens)] * 2
+        + [columns(wide), columns(wide), pl.BlockSpec((tile, wide), lambda i: (i, 0))],
+        out_specs=tuple([full(member) for member in out_shape[:5]] + [columns(tokens)] * 2),
+        scratch_shapes=[
+            pltpu.VMEM((tokens, wide), high),
+            pltpu.VMEM((tokens, heads * HEAD), low),
+            pltpu.VMEM((tokens, split), high),
+            pltpu.VMEM((tokens, w_qkv.shape[1] - split), high),
+        ],
+        compiler_params=pltpu.CompilerParams(vmem_limit_bytes=56 * 2**20),
+        cost_estimate=pl.CostEstimate(
+            flops=24 * 2**28, bytes_accessed=36 * 2**20, transcendentals=2**20
+        ),
+        name="backward_layer",
+    )(*ins, gate_pre, up_pre, w_gate, w_up, w_down)
+
+
+def widen(array, members, room):
+    width = array.shape[-1] // members
+    cut = array.reshape(array.shape[:-1] + (members, width))
+    cut = jnp.pad(cut, [(0, 0)] * (cut.ndim - 1) + [(0, room - width)])
+    return cut.reshape(array.shape[:-1] + (members * room,))
+
+
+def narrow(array, members, width):
+    room = array.shape[-1] // members
+    cut = array.reshape(array.shape[:-1] + (members, room))[..., :width]
+    return cut.reshape(array.shape[:-1] + (members * width,))
+
+
+def lifted(array, height, width):
+    return jnp.pad(array, [(0, height - array.shape[0]), (0, width - array.shape[1])])
+
+
+def rows_room(model, members):
+    return -(-(model // members + 1) // 16) * 16
+
+
+def on_device_fast(boundary, doc_lens, w_query, w_key, w_value, w_out, gains, w_gate, w_up, w_down):
+    section = lax.axis_index("section")
+    members = lax.axis_size("dp")
+    _, micro_count, rows, model = boundary.shape
+    tokens = micro_count * rows
+    piece = model // members
+    room = rows_room(model, members)
+    wide = room * members
+    kv_width = w_key.size // piece
+    hidden = w_gate.size // piece
+    heads, kv_heads = model // HEAD, kv_width // HEAD
+    layout = (heads, kv_heads, micro_count, rows)
+    split = model + kv_width
+    qkv_wide = split + -(-kv_width // 128) * 128
+    hidden_piece = hidden // members
+    gain_piece = gains.size
+
+    feature = jnp.arange(model, dtype=jnp.int32)
+    spread = (
+        (feature // piece * room + feature % piece)[:, None]
+        == jnp.arange(wide, dtype=jnp.int32)[None, :]
+    ).astype(jnp.bfloat16)
+
+    def spread_out(array):
+        return jnp.dot(array, spread, preferred_element_type=jnp.float32).astype(array.dtype)
+
+    qkv_piece = jnp.concatenate(
+        [
+            w_query.reshape(piece, model),
+            w_key.reshape(piece, kv_width),
+            w_value.reshape(piece, kv_width),
+        ],
+        axis=1,
+    )
+    out_piece = lifted(spread_out(w_out.reshape(piece, model)), room, wide)
+    gain_row = lifted(gains.reshape(1, gain_piece), 1, wide)
+    out_piece = lax.dynamic_update_slice(out_piece, gain_row, (piece, 0))
+    gathered = gather_all(
+        (
+            lifted(qkv_piece, room, qkv_wide),
+            out_piece,
+            lifted(w_gate.reshape(piece, hidden), room, hidden),
+            lifted(w_up.reshape(piece, hidden), room, hidden),
+            spread_out(w_down.reshape(hidden_piece, model)),
+        ),
+        members,
+    )
+    gain_rows = gathered[1].reshape(members, room, wide)[:, piece, :gain_piece]
+    gain_pair = widen(gain_rows.reshape(2, model), members, room).astype(jnp.float32)
+
+    layouts = [doc_layout(doc_lens[micro, 0], rows) for micro in range(micro_count)]
+    segments = jnp.stack([item[0] for item in layouts])
+    positions = jnp.concatenate([item[1] for item in layouts])
+    live = jnp.concatenate([item[2] for item in layouts]).astype(jnp.float32)
+    slot_ids = jnp.arange(rows, dtype=jnp.int32)
+    allowed = (slot_ids[None, :] <= slot_ids[:, None])[None] & (
+        segments[:, :, None] == segments[:, None, :]
+    )
+    bias = jnp.where(allowed, 0.0, -1e30).astype(jnp.float32)
+    cos_table, sine_table = rope_tables(positions)
+    first_half = (jnp.arange(HEAD, dtype=jnp.int32) < HEAD // 2)[None, :]
+    repeat = split // HEAD
+    tables = tuple(
+        jnp.tile(table, (1, repeat))
+        for table in (
+            cos_table,
+            jnp.where(first_half, -sine_table, 0.0),
+            jnp.where(first_half, 0.0, sine_table),
+        )
+    )
+
+    own = spread_out(boundary.reshape(tokens, model))
+    stream_zero = own.astype(jnp.float32)
+    shared = (gain_pair, bias, tables, spread, gathered)
+    kept_zero = forward_fast(model, layout, stream_zero, *shared)
+    relayed = passed_along(kept_zero[0].astype(jnp.bfloat16), "section", 1)
+    stream_one = relayed.astype(jnp.float32)
+    kept_one = forward_fast(model, layout, stream_one, *shared)
+
+    cotangent = jnp.where(section == 1, stream_zero * live[:, None], 0.0)
+    back_one = backward_fast(model, layout, cotangent, (stream_one,) + tuple(kept_one[1:]), *shared)
+    returned = passed_along(back_one[0].astype(jnp.bfloat16), "section", -1).astype(jnp.float32)
+    back_zero = backward_fast(
+        model, layout, returned, (stream_zero,) + tuple(kept_zero[1:]), *shared
+    )
+
+    pick = lambda early, late: jnp.where(section == 0, early, late)
+    results = narrow(pick(back_zero[0], kept_one[0]), members, piece)
+    normed, mixed, normed_two, activation = (
+        pick(kept_zero[at], kept_one[at]) for at in (1, 4, 6, 9)
+    )
+    _, grad_low, grad_gains, grad_branch, grad_qkv, grad_gate, grad_up = (
+        pick(early, late) for early, late in zip(back_zero, back_one)
+    )
+    product = lambda left, right: jnp.einsum(
+        "nd,ne->de", left, right, preferred_element_type=jnp.float32
+    ).astype(jnp.bfloat16)
+    gain_terms = narrow(grad_gains, members, piece).reshape(members, 1, gain_piece)
+    out_terms = lax.dynamic_update_slice(
+        product(mixed, grad_branch).reshape(members, room, wide),
+        gain_terms.astype(jnp.bfloat16),
+        (0, piece, 0),
+    ).reshape(wide, wide)
+    share_qkv, share_out, share_gate, share_up, share_down = scatter_all(
+        (
+            product(normed, grad_qkv),
+            out_terms,
+            product(normed_two, grad_gate),
+            product(normed_two, grad_up),
+            product(activation, grad_low),
+        ),
+        members,
+    )
+    flat = lambda array: array.reshape(1, -1)
+    return (
+        results.reshape(1, micro_count, rows, model),
+        flat(share_qkv[:piece, :model]),
+        flat(share_qkv[:piece, model:split]),
+        flat(share_qkv[:piece, split : split + kv_width]),
+        flat(narrow(share_out[:piece], members, piece)),
+        flat(share_out[piece : piece + 1, :gain_piece]),
+        flat(share_gate[:piece]),
+        flat(share_up[:piece]),
+        flat(narrow(share_down, members, piece)),
+    )
+
+
+def rows_fit(mesh, model, hidden):
+    members = mesh.shape["dp"]
+    return (
+        mesh.shape["section"] == 2
+        and members >= 6
+        and members % 4 == 0
+        and model % members == 0
+        and hidden % members == 0
+        and (hidden // members) % 16 == 0
+        and (rows_room(model, members) * members) % 128 == 0
+    )
+
+
 def solution(mesh):
     placed = (
         P("section", None, "dp", None),
@@ -436,8 +1129,14 @@
         P("section", "dp"),
         P("section", "dp"),
     )
+
+    def chosen(*operands):
+        model = operands[0].shape[3]
+        hidden = operands[7].size * mesh.shape["dp"] // model
+        return (on_device_fast if rows_fit(mesh, model, hidden) else on_device)(*operands)
+
     return jax.shard_map(
-        on_device,
+        chosen,
         mesh=mesh,
         in_specs=placed,
         out_specs=(

time: 1370 us -> 442 us (0.32); the launches traced: 1350 us -> 438 us
  other arithmetic: 671 us -> 34.9 us
  Pallas kernels: 0 us -> 317 us
  matrix products: 251 us -> 23.8 us
  local copies, waits for them, and re-layouts: 235 us -> 29.8 us
  blocking collectives: 73.4 us -> 0 us
  starting transfers between devices: 60.9 us -> 4.76 us
  waiting for transfers between devices: 42.6 us -> 25.7 us
  between operations: 16.8 us -> 1.68 us
    pallas_call x0 -> x6, Pallas kernels: none -> 317 us  [the longest x1 109 us: scatter_all(): pl.pallas_call(functools.partial(scatter_kernel, chips, heights), out_sha...]
    convert_element_type x39 -> x7, other arithmetic: 302 us -> 6.45 us  [the longest x1 1.64 us: on_device_fast(): spread = ((feature // piece * room + feature % piece)[:, None] == jnp.ara...]
    all_gather x7 -> x0, other arithmetic: 292 us -> none  [the longest x1 75.9 us: on_device(): lax.all_gather(shards[6], 'dp', axis=0, tiled=True)]
    dot_general x168 -> x8, matrix products: 251 us -> 23.8 us  [the longest x5 18.9 us: on_device_fast(): jnp.einsum('nd,ne->de', left, right, preferred_element_type=jnp.float32)]
    unnamed x352 -> x59, local copies, waits for them, and re-layouts: 113 us -> 5.28 us
    all_gather x3 -> x0, blocking collectives: 73.4 us -> none  [the longest x1 28.8 us: on_device(): lax.all_gather(shards[2], 'dp', axis=0, tiled=True)]
    convert_element_type x13 -> x2, local copies, waits for them, and re-layouts: 56.9 us -> 0.77 us  [the longest x1 0.68 us: on_device_fast(): widen(gain_rows.reshape(2, model), members, room).astype(jnp.float32)]
    reduce_sum x26 -> x0, other arithmetic: 52.7 us -> none  [the longest x8 51.4 us: add_sources(): jnp.sum(member, axis=0, keepdims=True)]
  transfers between devices with their start and end apart: 17 -> 2, of which waited for: 6 -> 2; matrix products, arithmetic and copies ran while one was open for 61% -> 0% of each run, Pallas kernels for 0% -> 0%
where the time goes in v1:
time: 442 us; the launch traced here: 438 us
  Pallas kernels  317 us (72%)
  other arithmetic  34.9 us (8%)
  local copies, waits for them, and re-layouts  29.8 us (7%)
  waiting for transfers between devices  25.7 us (6%)
  matrix products  23.8 us (5%)
  starting transfers between devices  4.76 us (1%)
    pallas_call x1, Pallas kernels, scatter_all(): pl.pallas_call(functools.partial(scatter_kernel, chips, heights), out_sha...  109 us
    pallas_call x1, Pallas kernels, gather_all(): pl.pallas_call(functools.partial(gather_kernel, chips, heights), out_shap...  109 us
    pallas_call x2, Pallas kernels, backward_fast(): pl.pallas_call(functools.partial(backward_kernel, model, layout), grid=(h...  55.2 us
    pallas_call x2, Pallas kernels, forward_fast(): pl.pallas_call(functools.partial(forward_kernel, model, layout), grid=(hi...  44.1 us
    ppermute x2, waiting for transfers between devices, passed_along(): return lax.ppermute(x, axis, pairs)  25.7 us
    unnamed x7, other arithmetic  23.8 us
    dot_general x5, matrix products, on_device_fast(): jnp.einsum('nd,ne->de', left, right, preferred_element_type=jnp.float32)  18.9 us
  transfers between devices with their start and end apart: 2, of which 2 were waited for; matrix products, arithmetic and copies ran while one was open for 0% of the time, Pallas kernels for 0%

profile of v1, /device:TPU:0, one launch (start us, length us, event | category | flops | bytes accessed | tf_op | source)
XLA Modules:
  0.0 438.0 jit_solution(4228715527329965383)
XLA Ops:
  0.7 0.7 slice_bitcast_fusion.3
  3.8 1.4 pad_add_fusion.1
  5.4 1.1 reduce.1
  6.6 1.1 reduce.2
  8.0 1.6 reduce
  12.1 1.6 fusion.spread
  13.7 0.8 fusion.19
  14.6 6.6 %reduce.4 = bf16[153600]{0:T(1024)(128)(2,1)S(1)} reduce(bf16[1,153600]{1,0:T(2,128)(2,1)S(1)} %copy-done.16, bf16[]{:T(256)} %constant.70), dimensions={0}, to_apply=%param.17.reduce_sub_computation | reduce | bytes 614402 | tf_op args[7]
  21.5 0.7 pad.26.refs_2_
  22.3 6.4 %reduce.5 = bf16[153600]{0:T(1024)(128)(2,1)S(1)} reduce(bf16[1,153600]{1,0:T(2,128)(2,1)S(1)} %copy-done.17, bf16[]{:T(256)} %constant.70), dimensions={0}, to_apply=%param.18.reduce_sub_computation | reduce | bytes 614402 | tf_op args[8]
  29.0 0.7 pad.27.refs_3_
  29.8 6.4 %reduce.6 = bf16[153600]{0:T(1024)(128)(2,1)S(1)} reduce(bf16[1,153600]{1,0:T(2,128)(2,1)S(1)} %copy-done.18, bf16[]{:T(256)} %constant.70), dimensions={0}, to_apply=%param.19.reduce_sub_computation | reduce | bytes 614402 | tf_op args[9]
  36.4 1.7 fusion.17.refs_4_
  38.8 1.5 copy.43.late_sine
  40.4 1.5 copy.41.cos_table
  42.0 1.5 copy.42.early_sine
  44.6 109.0 %gather_ring.1 = (bf16[1024,1664]{1,0:T(8,128)(2,1)}, bf16[1024,1024]{1,0:T(8,128)(2,1)}, bf16[1024,2560]{1,0:T(8,128)(2,1)}, bf16[1024,2560]{1,0:T(8,128)(2,1)}, bf16[2560,1024]{1,0:T(8,128)(2,1)}) custom-call(bf16[64,1664]{1,0:T(8,128)(2,1)} %pad.23.refs_0_, bf16[64,1024]{1,0:T(8,128)(2,1)} %copy-done.21, bf16[64,2560]{1,0:T(8,128)(2,1)} %pad.26.refs_2_, ...), custom_call_target="tpu_custom_call" | custom-call | tf_op jit(solution)/shard_map/gather_ring/pallas_call | solution.py:527
  153.6 0.8 slice.73
  155.2 0.8 and_select_fusion.bias
  155.9 2.4 multiply_select_fusion
  158.3 22.0 %forward_layer.2 = (f32[256,1024]{1,0:T(8,128)}, bf16[256,1024]{1,0:T(8,128)(2,1)}, bf16[256,1280]{1,0:T(8,128)(2,1)}, bf16[256,384]{1,0:T(8,128)(2,1)}, bf16[25...) custom-call(f32[256,1024]{1,0:T(8,128)} %get-tuple-element.126.strea, ...), custom_call_target="tpu_custom_call" | custom-call | flops 5368709120 | bytes 31457280 | tf_op jit(solution)/shard_map/forward_layer/pallas_call | solution.py:790
  180.4 1.3 convert_element_type.118
  181.7 3.5 collective-permute-start
  185.1 11.6 %collective-permute-done = bf16[256,1024]{1,0:T(8,128)(2,1)S(1)} collective-permute-done((bf16[256,1024]{1,0:T(8,128)(2,1)S(1)}, bf16[256,1024]{1,0:T(8,128)(2,1)S(1)}, u32[]{:S(2)}, u32[]{:S(2)}) %collective-permute-start) | collective-permute-done | bytes 524320 | tf_op jit(solution)/shard_map/ppermute | solution.py:20
  196.8 1.1 convert_element_type.119.stream
  197.9 22.1 %forward_layer.3 = (f32[256,1024]{1,0:T(8,128)}, bf16[256,1024]{1,0:T(8,128)(2,1)}, bf16[256,1280]{1,0:T(8,128)(2,1)}, bf16[256,384]{1,0:T(8,128)(2,1)}, bf16[25...) custom-call(f32[256,1024]{1,0:T(8,128)} %convert_element_type.119.st, ...), custom_call_target="tpu_custom_call" | custom-call | flops 5368709120 | bytes 31457280 | tf_op jit(solution)/shard_map/forward_layer/pallas_call | solution.py:790
  220.0 27.6 %backward_layer.2 = (f32[256,1024]{1,0:T(8,128)}, bf16[256,1024]{1,0:T(8,128)(2,1)}, f32[2,1024]{1,0:T(2,128)}, bf16[256,1024]{1,0:T(8,128)(2,1)}, bf16[256,1664...) custom-call(f32[256,1024]{1,0:T(8,128)} %get-tuple-element.125.cotangent, ...), custom_call_target="tpu_custom_call" | custom-call | flops 6442450944 | bytes 37748736 | tf_op jit(solution)/shard_map/backward_layer/pallas_call | solution.py:936
  247.5 1.3 convert_element_type.120
  248.8 1.3 collective-permute-start.1
  250.1 14.1 %collective-permute-done.1 = bf16[256,1024]{1,0:T(8,128)(2,1)S(1)} collective-permute-done((bf16[256,1024]{1,0:T(8,128)(2,1)S(1)}, bf16[256,1024]{1,0:T(8,128)(2,1)S(1)}, u32[]{:S(2)}, u32[]{:S(2)}) %collective-permute-start.1) | collective-permute-done | bytes 524320 | tf_op jit(solution)/shard_map/ppermute | solution.py:20
  264.2 1.1 convert_element_type.121.cotangent
  265.3 27.6 %backward_layer.3 = (f32[256,1024]{1,0:T(8,128)}, bf16[256,1024]{1,0:T(8,128)(2,1)}, f32[2,1024]{1,0:T(2,128)}, bf16[256,1024]{1,0:T(8,128)(2,1)}, bf16[256,1664...) custom-call(f32[256,1024]{1,0:T(8,128)} %convert_element_type.121.cotangent, ...), custom_call_target="tpu_custom_call" | custom-call | flops 6442450944 | bytes 37748736 | tf_op jit(solution)/shard_map/backward_layer/pallas_call | solution.py:936
  293.8 2.1 convolution_convert_fusion.4
  296.6 6.0 %convolution_convert_fusion.2.refs_2_ = bf16[1024,2560]{1,0:T(8,128)(2,1)} fusion(bf16[256,2560]{1,0:T(8,128)(2,1)} %get-tuple-element.84, bf16[256,2560]{1,0:T(8,128)(2,1)} %get-tuple-element.85, pred[]{:T(512)S(6)} %eq.106, bf16[256,1024]{1,0:T(8,128)(2,1)S(1)} %copy-done.3, bf16[256,1024]{1,0:T(8,128)(2,1)S(1)} %copy-done.4), kind=kOutput, calls=%fused_computation.2 | convolution fusion | flops 1345716224 | bytes 8912897 | tf_op jit(solution)/shard_map/nd,ne->de/dot_general | solution.py:1073
  302.6 3.9 convolution_convert_fusion.1.refs_3_
  306.6 3.0 convolution_convert_fusion.3.refs_0_
  309.6 3.9 convolution_convert_fusion.refs_4_
  313.6 109.1 %scatter_ring.1 = (f32[64,1664]{1,0:T(8,128)}, f32[64,1024]{1,0:T(8,128)}, f32[64,2560]{1,0:T(8,128)}, f32[64,2560]{1,0:T(8,128)}, f32[160,1024]{1,0:T(8,128)}) custom-call(bf16[1024,1664]{1,0:T(8,128)(2,1)} %convolution_convert_fusion.3.refs_0_, bf16[1024,1024]{1,0:T(8,128)(2,1)} %bitcast.59, bf16[1024,2560]{1,0:T(8,128)(2,1)} %convolution_convert_fusion.2.refs_2_, ...), custom_call_target="tpu_custom_call" | custom-call | tf_op jit(solution)/shard_map/scatter_ring/pallas_call | solution.py:624
  422.6 1.1 fusion.43
  423.7 1.0 slice.64
  425.7 1.0 copy.55
  426.8 1.5 copy.59
  428.8 1.0 reshape.292
  429.7 0.8 reshape.294
  430.5 0.8 reshape.293
  431.4 1.4 reshape_reshape.11
  432.8 1.5 copy.60
  434.6 2.9 reshape_reshape.12
  (107 shorter events, 13.0 us)
Async XLA Ops:
  0.6 10.6 %copy-start.24 = (bf16[1,57600]{1,0:T(2,128)(2,1)S(1)}, bf16[1,57600]{1,0:T(2,128)(2,1)}, u32[]{:S(2)}) copy-start(bf16[1,57600]{1,0:T(2,128)(2,1)} %param.15) | copy-start | bytes 345604
  11.3 3.3 copy-start.16
  13.7 8.5 %copy-start.17 = (bf16[1,153600]{1,0:T(2,128)(2,1)S(1)}, bf16[1,153600]{1,0:T(2,128)(2,1)}, u32[]{:S(2)}) copy-start(bf16[1,153600]{1,0:T(2,128)(2,1)} %param.18) | copy-start | bytes 921604
  14.6 15.2 %copy-start.18 = (bf16[1,153600]{1,0:T(2,128)(2,1)S(1)}, bf16[1,153600]{1,0:T(2,128)(2,1)}, u32[]{:S(2)}) copy-start(bf16[1,153600]{1,0:T(2,128)(2,1)} %param.19) | copy-start | bytes 921604
  29.0 9.1 %copy-start.22 = (bf16[1,2,128,960]{2,3,1,0:T(8,128)(2,1)S(1)}, bf16[1,2,128,960]{2,3,1,0:T(8,128)(2,1)}, u32[]{:S(2)}) copy-start(bf16[1,2,128,960]{2,3,1,0:T(8,128)(2,1)} %param.10) | copy-start | bytes 1474564
  44.0 0.7 copy-start.21
  181.7 15.1 %collective-permute-start = (bf16[256,1024]{1,0:T(8,128)(2,1)S(1)}, bf16[256,1024]{1,0:T(8,128)(2,1)S(1)}, u32[]{:S(2)}, u32[]{:S(2)}) collective-permute-start(bf16[256,1024]{1,0:T(8,128)(2,1)S(1)} %convert_element_type.118), channel_id=1, source_target_pairs={{0,16},{1,17},{2,18},{3,19},{4,20},{5,21},{6,22},{7,23},{8,24},{9,... | collective-permute-start | bytes 1572872 | tf_op jit(solution)/shard_map/ppermute | solution.py:20
  248.8 15.4 %collective-permute-start.1 = (bf16[256,1024]{1,0:T(8,128)(2,1)S(1)}, bf16[256,1024]{1,0:T(8,128)(2,1)S(1)}, u32[]{:S(2)}, u32[]{:S(2)}) collective-permute-start(bf16[256,1024]{1,0:T(8,128)(2,1)S(1)} %convert_element_type.120), channel_id=1, source_target_pairs={{16,0},{17,1},{18,2},{19,3},{20,4},{21,5},{22,6},{23,7},{24,8},{25... | collective-permute-start | bytes 1572872 | tf_op jit(solution)/shard_map/ppermute | solution.py:20
  265.3 27.6 %copy-start.25 = (f32[2,1024]{1,0:T(2,128)S(1)}, f32[2,1024]{1,0:T(2,128)}, u32[]{:S(2)}) copy-start(f32[2,1024]{1,0:T(2,128)} %get-tuple-element.81) | copy-start | bytes 24580
  293.8 2.7 copy-start.3
  293.8 2.7 copy-start.4
  296.5 6.0 %copy-start = (bf16[16,64,1024]{2,1,0:T(8,128)(2,1)}, bf16[16,64,1024]{2,1,0:T(8,128)(2,1)S(1)}, u32[]{:S(2)}) copy-start(bf16[16,64,1024]{2,1,0:T(8,128)(2,1)S(1)} %dynamic_update_slice.7) | copy-start | bytes 6291460
  296.6 6.0 %copy-start.7 = (bf16[256,2560]{1,0:T(8,128)(2,1)S(1)}, bf16[256,2560]{1,0:T(8,128)(2,1)}, u32[]{:S(2)}) copy-start(bf16[256,2560]{1,0:T(8,128)(2,1)} %get-tuple-element.87) | copy-start | bytes 3932164
  296.6 6.0 %copy-start.8 = (bf16[256,2560]{1,0:T(8,128)(2,1)S(1)}, bf16[256,2560]{1,0:T(8,128)(2,1)}, u32[]{:S(2)}) copy-start(bf16[256,2560]{1,0:T(8,128)(2,1)} %get-tuple-element.86) | copy-start | bytes 3932164
  302.6 4.0 copy-start.5
  302.6 4.0 copy-start.6
  302.6 4.0 copy-start.11
  302.6 3.9 copy-start.12
  306.6 3.1 copy-start.1
  306.6 3.0 copy-start.2
  306.6 3.0 copy-start.19
  306.6 3.0 copy-start.20
  313.6 111.1 %copy-start.9 = (f32[256,1024]{1,0:T(8,128)S(1)}, f32[256,1024]{1,0:T(8,128)}, u32[]{:S(2)}) copy-start(f32[256,1024]{1,0:T(8,128)} %get-tuple-element.71) | copy-start | bytes 3145732
  313.6 111.1 %copy-start.10 = (f32[256,1024]{1,0:T(8,128)S(1)}, f32[256,1024]{1,0:T(8,128)}, u32[]{:S(2)}) copy-start(f32[256,1024]{1,0:T(8,128)} %get-tuple-element.70) | copy-start | bytes 3145732
  425.2 1.5 copy-start.14
  425.7 2.5 copy-start.23
  426.8 5.9 %copy-start.13 = (f32[64,2560]{1,0:T(8,128)S(1)}, f32[64,2560]{1,0:T(8,128)}, u32[]{:S(2)}) copy-start(f32[64,2560]{1,0:T(8,128)} %get-tuple-element.95) | copy-start | bytes 1966084
  430.5 3.8 copy-start.15

commit v2 on v1

--- a/solution.py
+++ b/solution.py
@@ -465,11 +465,61 @@
     return member, core, turn, at, following, sibling
 
 
-def gather_kernel(chips, heights, *refs):
-    count = len(heights)
-    pieces = refs[:count]
-    wholes = refs[count : 2 * count]
-    keep_sem, ring_send, ring_recv, side_send, side_recv = refs[2 * count :]
+def unit_of(width):
+    return 1 if width % 128 == 0 else 2
+
+
+def flat_part(line, width):
+    span = unit_of(width) * width
+    return pl.ds(pl.multiple_of(line * span, 128), span)
+
+
+def rows_from(flat, stage, count, width, lane):
+    unit = unit_of(width)
+
+    def body(line):
+        taken = flat[0:1, flat_part(line, width)].astype(jnp.float32)
+        for u in range(unit):
+            stage[pl.ds(line * unit + u, 1), lane : lane + width] = taken[
+                :, u * width : (u + 1) * width
+            ]
+
+    pl.loop(0, count // unit)(body)
+
+
+def rows_into(flat, stage, count, width, lane):
+    unit = unit_of(width)
+
+    def body(line):
+        taken = [stage[pl.ds(line * unit + u, 1), lane : lane + width] for u in range(unit)]
+        flat[0:1, flat_part(line, width)] = jnp.concatenate(taken, axis=1)
+
+    pl.loop(0, count // unit)(body)
+
+
+SEND_ORDER = (2, 3, 4, 0, 1)
+
+
+def gather_kernel(
+    chips,
+    sizes,
+    w_query,
+    w_key,
+    w_value,
+    w_out,
+    w_gate,
+    w_up,
+    w_down,
+    gain_row,
+    spread,
+    *refs,
+):
+    piece, hidden_piece, model, kv_width, hidden = sizes
+    wholes = refs[:5]
+    pieces = refs[5:10]
+    stage, keep_sem, ring_send, ring_recv, side_send, side_recv = refs[10:]
+    heights = [whole.shape[0] // (2 * chips) for whole in wholes]
+    room, wide = pieces[1].shape
     member, core, turn, at, following, sibling = ring_setup(chips)
 
     def rows(index, owner):
@@ -496,73 +546,105 @@
             device_id_type=pl.DeviceIdType.MESH,
         )
 
-    for index in range(count):
+    def keep_copy(index):
+        return pltpu.make_async_copy(pieces[index], rows(index, member), keep_sem.at[index])
+
+    def build(index):
+        if index == 0:
+            stage[:room, : pieces[0].shape[1]] = jnp.zeros(pieces[0].shape, jnp.float32)
+            rows_from(w_query, stage, piece, model, 0)
+            rows_from(w_key, stage, piece, kv_width, model)
+            rows_from(w_value, stage, piece, kv_width, model + kv_width)
+            pieces[0][...] = stage[:room, : pieces[0].shape[1]].astype(jnp.bfloat16)
+        elif index == 1:
+            stage[:room, :model] = jnp.zeros((room, model), jnp.float32)
+            rows_from(w_out, stage, piece, model, 0)
+            spaced = dot(stage[:room, :model].astype(jnp.bfloat16), spread[...])
+            line = lax.broadcasted_iota(jnp.int32, (room, wide), 0)
+            spaced = spaced + jnp.where(line == piece, gain_row[...], 0.0)
+            pieces[1][...] = spaced.astype(jnp.bfloat16)
+        elif index == 4:
+            rows_from(w_down, stage, hidden_piece, model, 0)
+            pieces[4][...] = dot(
+                stage[:hidden_piece, :model].astype(jnp.bfloat16), spread[...]
+            ).astype(jnp.bfloat16)
+        else:
+            stage[:room, :hidden] = jnp.zeros((room, hidden), jnp.float32)
+            rows_from(w_gate if index == 2 else w_up, stage, piece, hidden, 0)
+            pieces[index][...] = stage[:room, :hidden].astype(jnp.bfloat16)
+
+    for index in SEND_ORDER:
+        build(index)
         ring_copy(index, pieces[index], member, 0).start()
-    for index in range(count):
         side_copy(index, pieces[index], member, 0).start()
-        pltpu.make_async_copy(pieces[index], rows(index, member), keep_sem.at[index]).start()
+        keep_copy(index).start()
     for step in range(1, chips):
         owner = at(-turn * step, core)
-        for index in range(count):
+        for index in SEND_ORDER:
             ring_copy(index, rows(index, owner), owner, step - 1).wait_recv()
             if step < chips - 1:
                 ring_copy(index, rows(index, owner), owner, step).start()
             side_copy(index, rows(index, owner), owner, step).start()
-    for index in range(count):
-        pltpu.make_async_copy(pieces[index], rows(index, member), keep_sem.at[index]).wait()
+    for index in SEND_ORDER:
+        keep_copy(index).wait()
     for step in range(chips):
         owner = at(-turn * step, core)
         theirs = at(turn * step, 1 - core)
-        for index in range(count):
+        for index in SEND_ORDER:
             if step < chips - 1:
                 ring_copy(index, rows(index, owner), owner, step).wait_send()
             side_copy(index, rows(index, owner), owner, step).wait_send()
             side_copy(index, rows(index, theirs), theirs, step).wait_recv()
 
 
-def gather_all(pieces, members):
+def gather_all(operands, sizes, members, shapes):
     chips = members // 2
-    heights = tuple(piece.shape[0] for piece in pieces)
-    count = len(pieces)
+    piece, hidden_piece, model, kv_width, hidden = sizes
+    vmem = pl.BlockSpec(memory_space=pltpu.VMEM)
     return pl.pallas_call(
-        functools.partial(gather_kernel, chips, heights),
+        functools.partial(gather_kernel, chips, sizes),
         out_shape=tuple(
-            jax.ShapeDtypeStruct((members * piece.shape[0], piece.shape[1]), piece.dtype)
-            for piece in pieces
+            jax.ShapeDtypeStruct((members * height, width), jnp.bfloat16)
+            for height, width in shapes
         ),
-        in_specs=[pl.BlockSpec(memory_space=pl.ANY)] * count,
-        out_specs=tuple([pl.BlockSpec(memory_space=pl.ANY)] * count),
-        scratch_shapes=[pltpu.SemaphoreType.DMA((count,))]
-        + [pltpu.SemaphoreType.DMA((chips, count))] * 4,
-        compiler_params=pltpu.CompilerParams(collective_id=0, has_side_effects=True),
+        in_specs=[vmem] * len(operands),
+        out_specs=tuple([pl.BlockSpec(memory_space=pl.ANY)] * 5),
+        scratch_shapes=[pltpu.VMEM(shape, jnp.bfloat16) for shape in shapes]
+        + [pltpu.VMEM((max(shapes[0][0], hidden_piece), max(hidden, shapes[0][1])), jnp.float32)]
+        + [pltpu.SemaphoreType.DMA((5,))]
+        + [pltpu.SemaphoreType.DMA((chips, 5))] * 4,
+        compiler_params=pltpu.CompilerParams(
+            collective_id=0, has_side_effects=True, vmem_limit_bytes=56 * 2**20
+        ),
         name="gather_ring",
-    )(*pieces)
-
-
-def scatter_kernel(chips, heights, *refs):
-    count = len(heights)
-    terms = refs[:count]
-    totals = refs[count : 2 * count]
-    owns = refs[2 * count : 3 * count]
-    sides = refs[3 * count : 4 * count]
-    rings = refs[4 * count : 5 * count]
-    load_sem, ring_send, ring_recv, side_send, side_recv = refs[5 * count :]
+    )(*operands)
+
+
+def scatter_kernel(chips, sizes, *refs):
+    piece, hidden_piece, model, kv_width, hidden = sizes
+    lefts = refs[:5]
+    rights = refs[5:10]
+    gain_terms, spread = refs[10:12]
+    out_query, out_key, out_value, out_out, out_gains, out_gate, out_up, out_down = refs[12:20]
+    owns, outs, sides, rings = refs[20:25], refs[25:30], refs[30:35], refs[35:40]
+    stage, ring_send, ring_recv, side_send, side_recv = refs[40:]
+    heights = [own.shape[1] for own in owns]
+    widths = [own.shape[2] for own in owns]
+    room = heights[1]
     member, core, turn, at, following, sibling = ring_setup(chips)
 
-    def rows(index, owner):
+    def term(index, owner):
         height = heights[index]
-        return terms[index].at[pl.ds(pl.multiple_of(owner * height, 16), height), :]
-
-    def load(index, step):
-        owner = at(-turn * (step + 1), core)
-        return pltpu.make_async_copy(
-            rows(index, owner), owns[index].at[step], load_sem.at[step, index]
-        )
+        part = lefts[index][pl.ds(pl.multiple_of(owner * height, 16), height), :]
+        value = dot(part, rights[index][...])
+        if index == 1:
+            line = lax.broadcasted_iota(jnp.int32, value.shape, 0)
+            value = value + jnp.where(line == piece, gain_terms[owner], 0.0)
+        return value.astype(jnp.bfloat16)
 
     def side_copy(index, step):
-        owner = at(turn * (step + 1), 1 - core)
         return pltpu.make_async_remote_copy(
-            src_ref=rows(index, owner),
+            src_ref=outs[index].at[step % 2],
             dst_ref=sides[index].at[step],
             send_sem=side_send.at[step, index],
             recv_sem=side_recv.at[step, index],
@@ -580,13 +662,38 @@
             device_id_type=pl.DeviceIdType.MESH,
         )
 
+    def finish(index):
+        if index == 0:
+            rows_into(out_query, stage, piece, model, 0)
+            rows_into(out_key, stage, piece, kv_width, model)
+            rows_into(out_value, stage, piece, kv_width, model + kv_width)
+        elif index == 2:
+            rows_into(out_gate, stage, piece, hidden, 0)
+        elif index == 3:
+            rows_into(out_up, stage, piece, hidden, 0)
+        else:
+            height = heights[index]
+            total = stage[:height, : widths[index]]
+            if index == 1:
+                out_gains[...] = total[piece : piece + 1, : out_gains.shape[1]]
+            upper = total.astype(jnp.bfloat16)
+            lower = (total - upper.astype(jnp.float32)).astype(jnp.bfloat16)
+            stage[:height, :model] = dot_nt(upper, spread[...]) + dot_nt(lower, spread[...])
+            if index == 1:
+                rows_into(out_out, stage, piece, model, 0)
+            else:
+                rows_into(out_down, stage, hidden_piece, model, 0)
+
     for step in range(chips):
-        for index in range(count):
+        theirs = at(turn * (step + 1), 1 - core)
+        mine = at(-turn * (step + 1), core)
+        for index in SEND_ORDER:
+            if step > 1:
+                side_copy(index, step - 2).wait_send()
+            outs[index][step % 2] = term(index, theirs)
             side_copy(index, step).start()
-            load(index, step).start()
-    for step in range(chips):
-        for index in range(count):
-            load(index, step).wait()
+            owns[index][step] = term(index, mine)
+        for index in SEND_ORDER:
             side_copy(index, step).wait_recv()
             if step > 0:
                 ring_copy(index, step - 1).wait_recv()
@@ -601,43 +708,55 @@
                 if step < chips - 1:
                     owns[index][step, part, :] = total.astype(jnp.bfloat16)
                 else:
-                    totals[index][part, :] = total
+                    stage[part, : widths[index]] = total
 
             pl.loop(0, heights[index] // 16)(add)
             if step < chips - 1:
                 ring_copy(index, step).start()
+            else:
+                finish(index)
     for step in range(chips):
-        for index in range(count):
-            side_copy(index, step).wait_send()
+        for index in SEND_ORDER:
+            if step >= chips - 2:
+                side_copy(index, step).wait_send()
             if step < chips - 1:
                 ring_copy(index, step).wait_send()
 
 
-def scatter_all(terms, members):
+def scatter_all(lefts, rights, gain_terms, spread, sizes, members):
     chips = members // 2
-    heights = tuple(term.shape[0] // members for term in terms)
-    widths = tuple(term.shape[1] for term in terms)
-    count = len(terms)
-    stacks = lambda depth: [
-        pltpu.VMEM((depth, height, width), jnp.bfloat16) for height, width in zip(heights, widths)
+    piece, hidden_piece, model, kv_width, hidden = sizes
+    shapes = [
+        (left.shape[0] // members, right.shape[1]) for left, right in zip(lefts, rights)
     ]
+    stacks = lambda depth: [pltpu.VMEM((depth, *shape), jnp.bfloat16) for shape in shapes]
+    lengths = (
+        piece * model,
+        piece * kv_width,
+        piece * kv_width,
+        piece * model,
+        -(-2 * piece // 128) * 128,
+        piece * hidden,
+        piece * hidden,
+        hidden_piece * model,
+    )
+    vmem = pl.BlockSpec(memory_space=pltpu.VMEM)
     return pl.pallas_call(
-        functools.partial(scatter_kernel, chips, heights),
-        out_shape=tuple(
-            jax.ShapeDtypeStruct((height, width), jnp.float32)
-            for height, width in zip(heights, widths)
-        ),
-        in_specs=[pl.BlockSpec(memory_space=pl.ANY)] * count,
-        out_specs=tuple([pl.BlockSpec(memory_space=pltpu.VMEM)] * count),
+        functools.partial(scatter_kernel, chips, sizes),
+        out_shape=tuple(jax.ShapeDtypeStruct((1, length), jnp.float32) for length in lengths),
+        in_specs=[vmem] * 12,
+        out_specs=tuple([vmem] * 8),
         scratch_shapes=stacks(chips)
+        + stacks(2)
         + stacks(chips)
         + stacks(chips - 1)
-        + [pltpu.SemaphoreType.DMA((chips, count))] * 5,
+        + [pltpu.VMEM((max(shapes[0][0], hidden_piece), max(hidden, shapes[0][1])), jnp.float32)]
+        + [pltpu.SemaphoreType.DMA((chips, 5))] * 4,
         compiler_params=pltpu.CompilerParams(
-            collective_id=1, has_side_effects=True, vmem_limit_bytes=56 * 2**20
+            collective_id=1, has_side_effects=True, vmem_limit_bytes=60 * 2**20
         ),
         name="scatter_ring",
-    )(*terms)
+    )(*lefts, *rights, gain_terms, spread)
 
 
 def dot(left, right):
@@ -657,13 +776,21 @@
 
 
 def turn_heads(values, tables, sign):
-    width = values.shape[1]
     cos_table, early_sine, late_sine = tables
     half = HEAD // 2
-    return values * cos_table[...] + sign * (
-        pltpu.roll(values, width - half, 1) * early_sine[...]
-        + pltpu.roll(values, half, 1) * late_sine[...]
-    )
+    span = cos_table.shape[1]
+    turned = []
+    for start in range(0, values.shape[1], span):
+        part = values[:, start : start + span]
+        turned.append(
+            part * cos_table[...]
+            + sign
+            * (
+                pltpu.roll(part, span - half, 1) * early_sine[...]
+                + pltpu.roll(part, half, 1) * late_sine[...]
+            )
+        )
+    return jnp.concatenate(turned, axis=1)
 
 
 def head_rows(source, micro, rows, first, group):
@@ -1002,26 +1129,13 @@
     def spread_out(array):
         return jnp.dot(array, spread, preferred_element_type=jnp.float32).astype(array.dtype)
 
-    qkv_piece = jnp.concatenate(
-        [
-            w_query.reshape(piece, model),
-            w_key.reshape(piece, kv_width),
-            w_value.reshape(piece, kv_width),
-        ],
-        axis=1,
-    )
-    out_piece = lifted(spread_out(w_out.reshape(piece, model)), room, wide)
-    gain_row = lifted(gains.reshape(1, gain_piece), 1, wide)
-    out_piece = lax.dynamic_update_slice(out_piece, gain_row, (piece, 0))
+    sizes = (piece, hidden_piece, model, kv_width, hidden)
+    gain_row = lifted(gains, 1, wide).astype(jnp.float32)
     gathered = gather_all(
-        (
-            lifted(qkv_piece, room, qkv_wide),
-            out_piece,
-            lifted(w_gate.reshape(piece, hidden), room, hidden),
-            lifted(w_up.reshape(piece, hidden), room, hidden),
-            spread_out(w_down.reshape(hidden_piece, model)),
-        ),
+        (w_query, w_key, w_value, w_out, w_gate, w_up, w_down, gain_row, spread),
+        sizes,
         members,
+        ((room, qkv_wide), (room, wide), (room, hidden), (room, hidden), (hidden_piece, wide)),
     )
     gain_rows = gathered[1].reshape(members, room, wide)[:, piece, :gain_piece]
     gain_pair = widen(gain_rows.reshape(2, model), members, room).astype(jnp.float32)
@@ -1037,9 +1151,8 @@
     bias = jnp.where(allowed, 0.0, -1e30).astype(jnp.float32)
     cos_table, sine_table = rope_tables(positions)
     first_half = (jnp.arange(HEAD, dtype=jnp.int32) < HEAD // 2)[None, :]
-    repeat = split // HEAD
     tables = tuple(
-        jnp.tile(table, (1, repeat))
+        jnp.tile(table, (1, 128 // HEAD))
         for table in (
             cos_table,
             jnp.where(first_half, -sine_table, 0.0),
@@ -1065,41 +1178,26 @@
     pick = lambda early, late: jnp.where(section == 0, early, late)
     results = narrow(pick(back_zero[0], kept_one[0]), members, piece)
     normed, mixed, normed_two, activation = (
-        pick(kept_zero[at], kept_one[at]) for at in (1, 4, 6, 9)
+        pick(kept_zero[at], kept_one[at]).T for at in (1, 4, 6, 9)
     )
     _, grad_low, grad_gains, grad_branch, grad_qkv, grad_gate, grad_up = (
         pick(early, late) for early, late in zip(back_zero, back_one)
     )
-    product = lambda left, right: jnp.einsum(
-        "nd,ne->de", left, right, preferred_element_type=jnp.float32
-    ).astype(jnp.bfloat16)
     gain_terms = narrow(grad_gains, members, piece).reshape(members, 1, gain_piece)
-    out_terms = lax.dynamic_update_slice(
-        product(mixed, grad_branch).reshape(members, room, wide),
-        gain_terms.astype(jnp.bfloat16),
-        (0, piece, 0),
-    ).reshape(wide, wide)
-    share_qkv, share_out, share_gate, share_up, share_down = scatter_all(
-        (
-            product(normed, grad_qkv),
-            out_terms,
-            product(normed_two, grad_gate),
-            product(normed_two, grad_up),
-            product(activation, grad_low),
-        ),
+    gain_terms = jnp.pad(gain_terms, ((0, 0), (0, 0), (0, wide - gain_piece)))
+    shares = scatter_all(
+        (normed, mixed, normed_two, normed_two, activation),
+        (grad_qkv, grad_branch, grad_gate, grad_up, grad_low),
+        gain_terms,
+        spread,
+        sizes,
         members,
     )
-    flat = lambda array: array.reshape(1, -1)
     return (
         results.reshape(1, micro_count, rows, model),
-        flat(share_qkv[:piece, :model]),
-        flat(share_qkv[:piece, model:split]),
-        flat(share_qkv[:piece, split : split + kv_width]),
-        flat(narrow(share_out[:piece], members, piece)),
-        flat(share_out[piece : piece + 1, :gain_piece]),
-        flat(share_gate[:piece]),
-        flat(share_up[:piece]),
-        flat(narrow(share_down, members, piece)),
+        *shares[:4],
+        shares[4][:, :gain_piece],
+        *shares[5:],
     )
 
 
@@ -1112,6 +1210,9 @@
         and model % members == 0
         and hidden % members == 0
         and (hidden // members) % 16 == 0
+        and hidden % 128 == 0
+        and model % 64 == 0
+        and (model // members) % 2 == 0
         and (rows_room(model, members) * members) % 128 == 0
     )
 

time: 442 us -> 428 us (0.968)
  Pallas kernels: 317 us -> 342 us
  matrix products: 23.8 us -> 2.39 us
  other arithmetic: 34.9 us -> 19.7 us
  local copies, waits for them, and re-layouts: 29.8 us -> 25.2 us
    pallas_call x2, Pallas kernels: 218 us -> 245 us  [the longest x1 129 us: scatter_all(): pl.pallas_call(functools.partial(scatter_kernel, chips, sizes), out_shape...]
    unnamed x7 -> x0, other arithmetic: 23.8 us -> none
    dot_general x5 -> x0, matrix products: 18.9 us -> none  [on_device_fast(): jnp.einsum('nd,ne->de', left, right, preferred_element_type=jnp.float32)]
    unnamed x59 -> x57, local copies, waits for them, and re-layouts: 5.28 us -> 13.3 us
    select_n x1 -> x7, other arithmetic: 0.14 us -> 7.69 us  [on_device_fast(): pick = lambda early, late: jnp.where(section == 0, early, late)]
    another operation x8 -> x7, local copies, waits for them, and re-layouts: 9.03 us -> 2.38 us  [the longest x6 2.3 us: on_device_fast(): jnp.tile(table, (1, 128 // HEAD))]
    transpose x0 -> x4, local copies, waits for them, and re-layouts: none -> 4.51 us  [on_device_fast(): pick(kept_zero[at], kept_one[at])]
  transfers between devices with their start and end apart: 2 -> 2, of which waited for: 2 -> 2; matrix products, arithmetic and copies ran while one was open for 0% -> 1% of each run, Pallas kernels for 0% -> 0%
where the time goes in v2:
time: 428 us; the launch traced here: 420 us
  Pallas kernels  342 us (80%)
  local copies, waits for them, and re-layouts  25.2 us (6%)
  waiting for transfers between devices  24.5 us (6%)
  other arithmetic  19.7 us (5%)
  starting transfers between devices  4.97 us (1%)
    pallas_call x1, Pallas kernels, scatter_all(): pl.pallas_call(functools.partial(scatter_kernel, chips, sizes), out_shape...  129 us
    pallas_call x1, Pallas kernels, gather_all(): pl.pallas_call(functools.partial(gather_kernel, chips, sizes), out_shape=...  115 us
    pallas_call x2, Pallas kernels, backward_fast(): pl.pallas_call(functools.partial(backward_kernel, model, layout), grid=(h...  55.2 us
    pallas_call x2, Pallas kernels, forward_fast(): pl.pallas_call(functools.partial(forward_kernel, model, layout), grid=(hi...  41.9 us
    ppermute x2, waiting for transfers between devices, passed_along(): return lax.ppermute(x, axis, pairs)  24.5 us
    unnamed x57, local copies, waits for them, and re-layouts  13.3 us
  transfers between devices with their start and end apart: 2, of which 2 were waited for; matrix products, arithmetic and copies ran while one was open for 1% of the time, Pallas kernels for 0%

profile of v2, /device:TPU:0, one launch (start us, length us, event | category | flops | bytes accessed | tf_op | source)
XLA Modules:
  0.0 420.1 jit_solution(14739713491054006712)
XLA Ops:
  0.7 0.7 slice_bitcast_fusion.1
  2.3 0.6 slice.35
  2.9 0.7 bitcast_subtract_fusion.1
  3.8 1.4 pad_add_fusion.1
  5.4 1.3 pad_convert_fusion.1.gain_row
  6.9 0.8 copy.50.cos_table
  7.7 0.8 copy.52.late_sine
  8.5 0.8 copy.51.early_sine
  9.8 1.7 fusion.spread.refs_11_
  11.4 115.4 %gather_ring.1 = (bf16[1024,1664]{1,0:T(8,128)(2,1)}, bf16[1024,1024]{1,0:T(8,128)(2,1)}, bf16[1024,2560]{1,0:T(8,128)(2,1)}, bf16[1024,2560]{1,0:T(8,128)(2,1)}, bf16[2560,1024]{1,0:T(8,128)(2,1)}) custom-call(bf16[1,57600]{1,0:T(2,128)(2,1)} %w_query.1, bf16[1,19200]{1,0:T(2,128)(2,1)} %w_key.1, bf16[1,19200]{1,0:T(2,128)(2,1)} %w_value.1, ...), custom_call_target="tpu_custom_call" | custom-call | tf_op jit(solution)/shard_map/gather_ring/pallas_call | solution.py:604
  126.8 0.8 slice.40
  127.7 0.7 reshape.221.gains
  128.4 0.8 and_select_fusion.bias
  129.1 2.4 multiply_select_fusion
  131.5 20.9 %forward_layer.2 = (f32[256,1024]{1,0:T(8,128)}, bf16[256,1024]{1,0:T(8,128)(2,1)}, bf16[256,1280]{1,0:T(8,128)(2,1)}, bf16[256,384]{1,0:T(8,128)(2,1)}, bf16[25...) custom-call(f32[256,1024]{1,0:T(8,128)} %get-tuple-element.130.strea, ...), custom_call_target="tpu_custom_call" | custom-call | flops 5368709120 | bytes 31457280 | tf_op jit(solution)/shard_map/forward_layer/pallas_call | solution.py:917
  152.4 1.3 convert_element_type.79
  153.8 3.7 collective-permute-start
  157.4 11.4 %collective-permute-done = bf16[256,1024]{1,0:T(8,128)(2,1)S(1)} collective-permute-done((bf16[256,1024]{1,0:T(8,128)(2,1)S(1)}, bf16[256,1024]{1,0:T(8,128)(2,1)S(1)}, u32[]{:S(2)}, u32[]{:S(2)}) %collective-permute-start) | collective-permute-done | bytes 524320 | tf_op jit(solution)/shard_map/ppermute | solution.py:20
  168.9 1.1 convert_element_type.80.stream
  170.0 21.0 %forward_layer.3 = (f32[256,1024]{1,0:T(8,128)}, bf16[256,1024]{1,0:T(8,128)(2,1)}, bf16[256,1280]{1,0:T(8,128)(2,1)}, bf16[256,384]{1,0:T(8,128)(2,1)}, bf16[25...) custom-call(f32[256,1024]{1,0:T(8,128)} %convert_element_type.80.str, ...), custom_call_target="tpu_custom_call" | custom-call | flops 5368709120 | bytes 31457280 | tf_op jit(solution)/shard_map/forward_layer/pallas_call | solution.py:917
  191.2 1.5 copy.67.refs_4_
  192.7 1.0 copy.65.refs_2_.refs_3_
  193.7 27.6 %backward_layer.2 = (f32[256,1024]{1,0:T(8,128)}, bf16[256,1024]{1,0:T(8,128)(2,1)}, f32[2,1024]{1,0:T(2,128)}, bf16[256,1024]{1,0:T(8,128)(2,1)}, bf16[256,1664...) custom-call(f32[256,1024]{1,0:T(8,128)} %get-tuple-element.129.cotangent, ...), custom_call_target="tpu_custom_call" | custom-call | flops 6442450944 | bytes 37748736 | tf_op jit(solution)/shard_map/backward_layer/pallas_call | solution.py:1063
  221.3 1.4 convert_element_type.81
  222.7 1.3 collective-permute-start.1
  224.1 1.0 copy.64.refs_1_
  225.3 1.0 copy.63.refs_0_
  226.3 13.1 %collective-permute-done.1 = bf16[256,1024]{1,0:T(8,128)(2,1)S(1)} collective-permute-done((bf16[256,1024]{1,0:T(8,128)(2,1)S(1)}, bf16[256,1024]{1,0:T(8,128)(2,1)S(1)}, u32[]{:S(2)}, u32[]{:S(2)}) %collective-permute-start.1) | collective-permute-done | bytes 524320 | tf_op jit(solution)/shard_map/ppermute | solution.py:20
  239.4 1.1 convert_element_type.82.cotangent
  240.5 27.6 %backward_layer.3 = (f32[256,1024]{1,0:T(8,128)}, bf16[256,1024]{1,0:T(8,128)(2,1)}, f32[2,1024]{1,0:T(2,128)}, bf16[256,1024]{1,0:T(8,128)(2,1)}, bf16[256,1664...) custom-call(f32[256,1024]{1,0:T(8,128)} %convert_element_type.82.cotangent, ...), custom_call_target="tpu_custom_call" | custom-call | flops 6442450944 | bytes 37748736 | tf_op jit(solution)/shard_map/backward_layer/pallas_call | solution.py:1063
  268.1 1.4 broadcast_select_fusion.5
  270.4 1.0 copy.68
  271.6 2.0 broadcast_select_fusion.3.refs_9_
  273.6 1.2 broadcast_select_fusion.refs_8_
  274.8 0.6 copy-done
  275.8 1.2 broadcast_select_fusion.1.refs_7_
  277.4 0.8 broadcast_select_fusion.4.refs_6_
  278.3 1.1 broadcast_select_fusion.2.refs_5_
  279.3 0.7 pad.14.refs_10_
  280.0 129.5 %scatter_ring.1 = (f32[1,57600]{1,0:T(1,128)}, f32[1,19200]{1,0:T(1,128)}, f32[1,19200]{1,0:T(1,128)}, f32[1,57600]{1,0:T(1,128)}, f32[1,128]{1,0:T(1,128)}, /*i...) custom-call(bf16[1024,256]{1,0:T(8,128)(2,1)} %copy.63.refs_0_, bf16[1024,256]{1,0:T(8,128)(2,1)} %copy.64.refs_1_, ...), custom_call_target="tpu_custom_call" | custom-call | tf_op jit(solution)/shard_map/scatter_ring/pallas_call | solution.py:744
  409.5 1.7 copy.86
  411.2 1.5 copy.87
  412.8 1.5 copy.88
  414.3 1.6 copy.89
  415.9 1.2 copy.90
  417.2 0.8 copy.91
  418.0 0.8 copy.92
  418.8 0.8 copy.93
  (81 shorter events, 4.6 us)
Async XLA Ops:
  0.6 8.6 %copy-start.20 = (bf16[1,2,128,960]{2,3,1,0:T(8,128)(2,1)S(1)}, bf16[1,2,128,960]{2,3,1,0:T(8,128)(2,1)}, u32[]{:S(2)}) copy-start(bf16[1,2,128,960]{2,3,1,0:T(8,128)(2,1)} %param.10) | copy-start | bytes 1474564
  153.8 15.1 %collective-permute-start = (bf16[256,1024]{1,0:T(8,128)(2,1)S(1)}, bf16[256,1024]{1,0:T(8,128)(2,1)S(1)}, u32[]{:S(2)}, u32[]{:S(2)}) collective-permute-start(bf16[256,1024]{1,0:T(8,128)(2,1)S(1)} %convert_element_type.79), channel_id=1, source_target_pairs={{0,16},{1,17},{2,18},{3,19},{4,20},{5,21},{6,22},{7,23},{8,24},{9,... | collective-permute-start | bytes 1572872 | tf_op jit(solution)/shard_map/ppermute | solution.py:20
  170.0 21.0 %copy-start.4 = (bf16[256,2560]{1,0:T(8,128)(2,1)S(1)}, bf16[256,2560]{1,0:T(8,128)(2,1)}, u32[]{:S(2)}) copy-start(bf16[256,2560]{1,0:T(8,128)(2,1)} %get-tuple-element.81) | copy-start | bytes 3932164
  191.1 1.5 copy-start.17
  191.1 1.5 copy-start.19
  221.3 2.7 copy-start.14
  221.3 2.7 copy-start.18
  222.7 16.7 %collective-permute-start.1 = (bf16[256,1024]{1,0:T(8,128)(2,1)S(1)}, bf16[256,1024]{1,0:T(8,128)(2,1)S(1)}, u32[]{:S(2)}, u32[]{:S(2)}) collective-permute-start(bf16[256,1024]{1,0:T(8,128)(2,1)S(1)} %convert_element_type.81), channel_id=1, source_target_pairs={{16,0},{17,1},{18,2},{19,3},{20,4},{21,5},{22,6},{23,7},{24,8},{25... | collective-permute-start | bytes 1572872 | tf_op jit(solution)/shard_map/ppermute | solution.py:20
  224.0 1.1 copy-start.13
  224.0 1.2 copy-start.16
  240.5 27.6 %copy-start.5 = (f32[256,1024]{1,0:T(8,128)S(1)}, f32[256,1024]{1,0:T(8,128)}, u32[]{:S(2)}) copy-start(f32[256,1024]{1,0:T(8,128)} %get-tuple-element.74) | copy-start | bytes 3145732
  270.4 1.1 copy-start.21
  270.4 1.1 copy-start.22
  270.4 1.2 copy-start.12
  270.4 3.2 copy-start.3
  271.4 2.2 copy-start.1
  273.6 1.8 copy-start
  273.6 2.2 copy-start.2
  275.8 1.2 copy-start.11
  275.8 1.6 copy-start.15
  275.8 2.4 copy-start.7
  277.0 1.3 copy-start.6
  409.5 7.7 %copy-start.10 = (f32[1,153600]{1,0:T(1,128)S(1)}, f32[1,153600]{1,0:T(1,128)}, u32[]{:S(2)}) copy-start(f32[1,153600]{1,0:T(1,128)} %get-tuple-element.150) | copy-start | bytes 1843204
  409.5 8.5 %copy-start.9 = (f32[1,153600]{1,0:T(1,128)S(1)}, f32[1,153600]{1,0:T(1,128)}, u32[]{:S(2)}) copy-start(f32[1,153600]{1,0:T(1,128)} %get-tuple-element.151) | copy-start | bytes 1843204
  415.9 2.9 copy-start.8

commit v3 on v2

--- a/solution.py
+++ b/solution.py
@@ -620,22 +620,51 @@
     )(*operands)
 
 
-def scatter_kernel(chips, sizes, *refs):
-    piece, hidden_piece, model, kv_width, hidden = sizes
-    lefts = refs[:5]
-    rights = refs[5:10]
-    gain_terms, spread = refs[10:12]
-    out_query, out_key, out_value, out_out, out_gains, out_gate, out_up, out_down = refs[12:20]
-    owns, outs, sides, rings = refs[20:25], refs[25:30], refs[30:35], refs[35:40]
-    stage, ring_send, ring_recv, side_send, side_recv = refs[40:]
+LEFT_OF = (0, 1, 2, 2, 3)
+
+
+def scatter_kernel(chips, sizes, micro_count, *refs):
+    piece = sizes[0]
+    fetched = 9
+    choices = 2 * micro_count
+    sources = [refs[slot * choices : (slot + 1) * choices] for slot in range(fetched)]
+    refs = refs[fetched * choices :]
+    gain_terms = refs[0]
+    totals = refs[1:6]
+    loaded, lefts = refs[6:15], refs[15:19]
+    owns, outs, sides, rings = refs[19:24], refs[24:29], refs[29:34], refs[34:39]
+    load_sem, ring_send, ring_recv, side_send, side_recv = refs[39:]
+    rights = loaded[4:]
     heights = [own.shape[1] for own in owns]
-    widths = [own.shape[2] for own in owns]
-    room = heights[1]
+    section = lax.axis_index("section")
     member, core, turn, at, following, sibling = ring_setup(chips)
+
+    def load(slot, micro, late):
+        rows = sources[slot][0].shape[0]
+        return pltpu.make_async_copy(
+            sources[slot][late * micro_count + micro],
+            loaded[slot].at[pl.ds(micro * rows, rows), :],
+            load_sem.at[slot, micro],
+        )
+
+    def start_load(slot):
+        for micro in range(micro_count):
+
+            @pl.when(section == 0)
+            def _():
+                load(slot, micro, 0).start()
+
+            @pl.when(section != 0)
+            def _():
+                load(slot, micro, 1).start()
+
+    def wait_load(slot):
+        for micro in range(micro_count):
+            load(slot, micro, 0).wait()
 
     def term(index, owner):
         height = heights[index]
-        part = lefts[index][pl.ds(pl.multiple_of(owner * height, 16), height), :]
+        part = lefts[LEFT_OF[index]][pl.ds(pl.multiple_of(owner * height, 16), height), :]
         value = dot(part, rights[index][...])
         if index == 1:
             line = lax.broadcasted_iota(jnp.int32, value.shape, 0)
@@ -662,59 +691,61 @@
             device_id_type=pl.DeviceIdType.MESH,
         )
 
-    def finish(index):
-        if index == 0:
-            rows_into(out_query, stage, piece, model, 0)
-            rows_into(out_key, stage, piece, kv_width, model)
-            rows_into(out_value, stage, piece, kv_width, model + kv_width)
-        elif index == 2:
-            rows_into(out_gate, stage, piece, hidden, 0)
-        elif index == 3:
-            rows_into(out_up, stage, piece, hidden, 0)
-        else:
-            height = heights[index]
-            total = stage[:height, : widths[index]]
-            if index == 1:
-                out_gains[...] = total[piece : piece + 1, : out_gains.shape[1]]
-            upper = total.astype(jnp.bfloat16)
-            lower = (total - upper.astype(jnp.float32)).astype(jnp.bfloat16)
-            stage[:height, :model] = dot_nt(upper, spread[...]) + dot_nt(lower, spread[...])
-            if index == 1:
-                rows_into(out_out, stage, piece, model, 0)
-            else:
-                rows_into(out_down, stage, hidden_piece, model, 0)
-
-    for step in range(chips):
+    def prepare(index, step):
         theirs = at(turn * (step + 1), 1 - core)
         mine = at(-turn * (step + 1), core)
+        if step > 1:
+            side_copy(index, step - 2).wait_send()
+        outs[index][step % 2] = term(index, theirs)
+        side_copy(index, step).start()
+        owns[index][step] = term(index, mine)
+
+    def advance(index, step):
+        side_copy(index, step).wait_recv()
+        if step > 0:
+            ring_copy(index, step - 1).wait_recv()
+
+        def add(block):
+            part = pl.ds(pl.multiple_of(block * 16, 16), 16)
+            total = owns[index][step, part, :].astype(jnp.float32) + sides[index][
+                step, part, :
+            ].astype(jnp.float32)
+            if step > 0:
+                total = total + rings[index][step - 1, part, :].astype(jnp.float32)
+            if step < chips - 1:
+                owns[index][step, part, :] = total.astype(jnp.bfloat16)
+            else:
+                totals[index][part, :] = total
+
+        pl.loop(0, heights[index] // 16)(add)
+        if step < chips - 1:
+            ring_copy(index, step).start()
+
+    ready = []
+    for index in SEND_ORDER:
+        if LEFT_OF[index] not in ready:
+            start_load(LEFT_OF[index])
+            ready.append(LEFT_OF[index])
+        start_load(4 + index)
+    ready = []
+    waiting = None
+    for index in SEND_ORDER:
+        left = LEFT_OF[index]
+        if left not in ready:
+            wait_load(left)
+            lefts[left][...] = loaded[left][...].T
+            ready.append(left)
+        wait_load(4 + index)
+        prepare(index, 0)
+        if waiting is not None:
+            advance(waiting, 0)
+        waiting = index
+    advance(waiting, 0)
+    for step in range(1, chips):
         for index in SEND_ORDER:
-            if step > 1:
-                side_copy(index, step - 2).wait_send()
-            outs[index][step % 2] = term(index, theirs)
-            side_copy(index, step).start()
-            owns[index][step] = term(index, mine)
+            prepare(index, step)
         for index in SEND_ORDER:
-            side_copy(index, step).wait_recv()
-            if step > 0:
-                ring_copy(index, step - 1).wait_recv()
-
-            def add(block):
-                part = pl.ds(pl.multiple_of(block * 16, 16), 16)
-                total = owns[index][step, part, :].astype(jnp.float32) + sides[index][
-                    step, part, :
-                ].astype(jnp.float32)
-                if step > 0:
-                    total = total + rings[index][step - 1, part, :].astype(jnp.float32)
-                if step < chips - 1:
-                    owns[index][step, part, :] = total.astype(jnp.bfloat16)
-                else:
-                    stage[part, : widths[index]] = total
-
-            pl.loop(0, heights[index] // 16)(add)
-            if step < chips - 1:
-                ring_copy(index, step).start()
-            else:
-                finish(index)
+            advance(index, step)
     for step in range(chips):
         for index in SEND_ORDER:
             if step >= chips - 2:
@@ -723,13 +754,60 @@
                 ring_copy(index, step).wait_send()
 
 
-def scatter_all(lefts, rights, gain_terms, spread, sizes, members):
+def scatter_all(sources, gain_terms, sizes, members):
     chips = members // 2
-    piece, hidden_piece, model, kv_width, hidden = sizes
+    micro_count = len(sources[0]) // 2
+    wholes = [(micro_count * group[0].shape[0], group[0].shape[1]) for group in sources]
     shapes = [
-        (left.shape[0] // members, right.shape[1]) for left, right in zip(lefts, rights)
+        (wholes[LEFT_OF[index]][1] // members, wholes[4 + index][1]) for index in range(5)
     ]
     stacks = lambda depth: [pltpu.VMEM((depth, *shape), jnp.bfloat16) for shape in shapes]
+    vmem = pl.BlockSpec(memory_space=pltpu.VMEM)
+    flat_sources = [member for group in sources for member in group]
+    return pl.pallas_call(
+        functools.partial(scatter_kernel, chips, sizes, micro_count),
+        out_shape=tuple(jax.ShapeDtypeStruct(shape, jnp.float32) for shape in shapes),
+        in_specs=[pl.BlockSpec(memory_space=pl.ANY)] * len(flat_sources) + [vmem],
+        out_specs=tuple([vmem] * 5),
+        scratch_shapes=[pltpu.VMEM(whole, jnp.bfloat16) for whole in wholes]
+        + [pltpu.VMEM(whole[::-1], jnp.bfloat16) for whole in wholes[:4]]
+        + stacks(chips)
+        + stacks(2)
+        + stacks(chips)
+        + stacks(chips - 1)
+        + [pltpu.SemaphoreType.DMA((9, micro_count))]
+        + [pltpu.SemaphoreType.DMA((chips, 5))] * 4,
+        compiler_params=pltpu.CompilerParams(
+            collective_id=1, has_side_effects=True, vmem_limit_bytes=60 * 2**20
+        ),
+        name="scatter_ring",
+    )(*flat_sources, gain_terms)
+
+
+def flatten_kernel(sizes, *refs):
+    piece, hidden_piece, model, kv_width, hidden = sizes
+    totals, spread = refs[:5], refs[5]
+    out_query, out_key, out_value, out_out, out_gains, out_gate, out_up, out_down = refs[6:14]
+    stage = refs[14]
+    rows_into(out_gate, totals[2], piece, hidden, 0)
+    rows_into(out_up, totals[3], piece, hidden, 0)
+    rows_into(out_query, totals[0], piece, model, 0)
+    rows_into(out_key, totals[0], piece, kv_width, model)
+    rows_into(out_value, totals[0], piece, kv_width, model + kv_width)
+    out_gains[...] = totals[1][piece : piece + 1, : out_gains.shape[1]]
+    for index in (1, 4):
+        total = totals[index][...]
+        upper = total.astype(jnp.bfloat16)
+        lower = (total - upper.astype(jnp.float32)).astype(jnp.bfloat16)
+        stage[: total.shape[0], :] = dot_nt(upper, spread[...]) + dot_nt(lower, spread[...])
+        if index == 1:
+            rows_into(out_out, stage, piece, model, 0)
+        else:
+            rows_into(out_down, stage, hidden_piece, model, 0)
+
+
+def flatten_all(totals, spread, sizes):
+    piece, hidden_piece, model, kv_width, hidden = sizes
     lengths = (
         piece * model,
         piece * kv_width,
@@ -742,21 +820,14 @@
     )
     vmem = pl.BlockSpec(memory_space=pltpu.VMEM)
     return pl.pallas_call(
-        functools.partial(scatter_kernel, chips, sizes),
+        functools.partial(flatten_kernel, sizes),
         out_shape=tuple(jax.ShapeDtypeStruct((1, length), jnp.float32) for length in lengths),
-        in_specs=[vmem] * 12,
+        in_specs=[vmem] * 6,
         out_specs=tuple([vmem] * 8),
-        scratch_shapes=stacks(chips)
-        + stacks(2)
-        + stacks(chips)
-        + stacks(chips - 1)
-        + [pltpu.VMEM((max(shapes[0][0], hidden_piece), max(hidden, shapes[0][1])), jnp.float32)]
-        + [pltpu.SemaphoreType.DMA((chips, 5))] * 4,
-        compiler_params=pltpu.CompilerParams(
-            collective_id=1, has_side_effects=True, vmem_limit_bytes=60 * 2**20
-        ),
-        name="scatter_ring",
-    )(*lefts, *rights, gain_terms, spread)
+        scratch_shapes=[pltpu.VMEM((max(totals[1].shape[0], hidden_piece), model), jnp.float32)],
+        compiler_params=pltpu.CompilerParams(vmem_limit_bytes=40 * 2**20),
+        name="flatten_pieces",
+    )(*totals, spread)
 
 
 def dot(left, right):
@@ -819,6 +890,7 @@
     w_up,
     w_down,
     layer_out,
+    layer_low,
     normed,
     turned,
     values,
@@ -835,7 +907,7 @@
 
     @pl.when(pl.program_id(0) == 0)
     def _():
-        residual = stream[...]
+        residual = stream[...].astype(jnp.float32)
         scale = lax.rsqrt(jnp.sum(residual * residual, axis=1, keepdims=True) / model + EPSILON)
         normed[...] = (residual * scale * gains[0:1, :]).astype(jnp.bfloat16)
         products = dot(normed[...], w_qkv[...])
@@ -876,6 +948,10 @@
     activation[...] = active
     layer_out[...] += dot(active, w_down[...])
 
+    @pl.when(pl.program_id(0) == pl.num_programs(0) - 1)
+    def _():
+        layer_low[...] = layer_out[...].astype(jnp.bfloat16)
+
 
 def full(array):
     return pl.BlockSpec(array.shape, lambda i: (0,) * len(array.shape))
@@ -903,6 +979,7 @@
     out_shape = (
         shape_of(tokens, wide, high),
         shape_of(tokens, wide, low),
+        shape_of(tokens, wide, low),
         shape_of(tokens, split, low),
         shape_of(tokens, w_qkv.shape[1] - split, low),
         shape_of(tokens, wide, low),
@@ -920,11 +997,11 @@
         out_shape=out_shape,
         in_specs=[full(member) for member in ins]
         + [columns(wide), columns(wide), pl.BlockSpec((tile, wide), lambda i: (i, 0))],
-        out_specs=tuple([full(member) for member in out_shape[:7]] + [columns(tokens)] * 3),
+        out_specs=tuple([full(member) for member in out_shape[:8]] + [columns(tokens)] * 3),
         scratch_shapes=[pltpu.VMEM((tokens, heads * HEAD), low)],
         compiler_params=pltpu.CompilerParams(vmem_limit_bytes=56 * 2**20),
         cost_estimate=pl.CostEstimate(
-            flops=20 * 2**28, bytes_accessed=30 * 2**20, transcendentals=2**20
+            flops=10 * 2**28, bytes_accessed=28 * 2**20, transcendentals=2**20
         ),
         name="forward_layer",
     )(*ins, w_gate, w_up, w_down)
@@ -952,7 +1029,7 @@
     w_up,
     w_down,
     grad_input,
-    grad_low,
+    input_low,
     grad_gains,
     grad_branch,
     grad_qkv,
@@ -969,11 +1046,10 @@
 
     @pl.when(step == 0)
     def _():
-        grad_low[...] = cotangent[...].astype(jnp.bfloat16)
         norm_grad[...] = jnp.zeros_like(norm_grad)
 
     gate = gate_pre[...]
-    grad_act = dot_nt(grad_low[...], w_down[...])
+    grad_act = dot_nt(cotangent[...], w_down[...])
     sigmoid = jax.nn.sigmoid(gate)
     grad_gate[...] = (
         grad_act * up_pre[...] * sigmoid * (1.0 + gate * (1.0 - sigmoid))
@@ -989,7 +1065,7 @@
         gradient = norm_grad[...]
         grad_gains[1:2, :] = jnp.sum(gradient * centered, axis=0, keepdims=True)
         scaled = gradient * gains[1:2, :]
-        grad_middle = cotangent[...] + scale_two * (
+        grad_middle = cotangent[...].astype(jnp.float32) + scale_two * (
             scaled - centered * (jnp.sum(scaled * centered, axis=1, keepdims=True) / model)
         )
         grad_input[...] = grad_middle
@@ -1028,7 +1104,7 @@
         ).astype(jnp.bfloat16)
         grad_qkv[:, split:] = grad_values[...].astype(jnp.bfloat16)
         first_gradient = dot_nt(grad_qkv[...], w_qkv[...])
-        residual = stream[...]
+        residual = stream[...].astype(jnp.float32)
         scale = lax.rsqrt(jnp.sum(residual * residual, axis=1, keepdims=True) / model + EPSILON)
         first_centered = residual * scale
         grad_gains[0:1, :] = jnp.sum(first_gradient * first_centered, axis=0, keepdims=True)
@@ -1038,11 +1114,12 @@
             - first_centered
             * (jnp.sum(first_scaled * first_centered, axis=1, keepdims=True) / model)
         )
+        input_low[...] = grad_input[...].astype(jnp.bfloat16)
 
 
 def backward_fast(model, layout, cotangent, kept, gains, bias, tables, spread, matrices):
     w_qkv, w_out, w_gate, w_up, w_down = matrices
-    stream, _, turned, values, _, middle, _, gate_pre, up_pre, _ = kept
+    stream, _, _, turned, values, _, middle, _, gate_pre, up_pre, _ = kept
     heads, kv_heads, micro_count, rows = layout
     tokens, wide = stream.shape
     hidden = w_gate.shape[1]
@@ -1076,7 +1153,7 @@
         ],
         compiler_params=pltpu.CompilerParams(vmem_limit_bytes=56 * 2**20),
         cost_estimate=pl.CostEstimate(
-            flops=24 * 2**28, bytes_accessed=36 * 2**20, transcendentals=2**20
+            flops=12 * 2**28, bytes_accessed=30 * 2**20, transcendentals=2**20
         ),
         name="backward_layer",
     )(*ins, gate_pre, up_pre, w_gate, w_up, w_down)
@@ -1161,40 +1238,47 @@
     )
 
     own = spread_out(boundary.reshape(tokens, model))
-    stream_zero = own.astype(jnp.float32)
-    shared = (gain_pair, bias, tables, spread, gathered)
-    kept_zero = forward_fast(model, layout, stream_zero, *shared)
-    relayed = passed_along(kept_zero[0].astype(jnp.bfloat16), "section", 1)
-    stream_one = relayed.astype(jnp.float32)
-    kept_one = forward_fast(model, layout, stream_one, *shared)
-
-    cotangent = jnp.where(section == 1, stream_zero * live[:, None], 0.0)
-    back_one = backward_fast(model, layout, cotangent, (stream_one,) + tuple(kept_one[1:]), *shared)
-    returned = passed_along(back_one[0].astype(jnp.bfloat16), "section", -1).astype(jnp.float32)
-    back_zero = backward_fast(
-        model, layout, returned, (stream_zero,) + tuple(kept_zero[1:]), *shared
-    )
+    dimmed = jnp.where(section == 1, own * live[:, None].astype(jnp.bfloat16), 0.0)
+    alone = (heads, kv_heads, 1, rows)
+    micros = range(micro_count)
+    part = lambda array, micro: array[micro * rows : (micro + 1) * rows]
+    shared = [
+        (gain_pair, bias[m : m + 1], tuple(part(t, m) for t in tables), spread, gathered)
+        for m in micros
+    ]
+    streams_zero = [part(own, m) for m in micros]
+    kept_zero = [forward_fast(model, alone, streams_zero[m], *shared[m]) for m in micros]
+    streams_one = [passed_along(kept[1], "section", 1) for kept in kept_zero]
+    kept_one = [forward_fast(model, alone, streams_one[m], *shared[m]) for m in micros]
+    starts_one = [part(dimmed, m).astype(jnp.bfloat16) for m in micros]
+    back_one = [
+        backward_fast(model, alone, starts_one[m], (streams_one[m], *kept_one[m][1:]), *shared[m])
+        for m in micros
+    ]
+    starts_zero = [passed_along(back[1], "section", -1) for back in back_one]
+    back_zero = [
+        backward_fast(
+            model, alone, starts_zero[m], (streams_zero[m], *kept_zero[m][1:]), *shared[m]
+        )
+        for m in micros
+    ]
 
     pick = lambda early, late: jnp.where(section == 0, early, late)
-    results = narrow(pick(back_zero[0], kept_one[0]), members, piece)
-    normed, mixed, normed_two, activation = (
-        pick(kept_zero[at], kept_one[at]).T for at in (1, 4, 6, 9)
-    )
-    _, grad_low, grad_gains, grad_branch, grad_qkv, grad_gate, grad_up = (
-        pick(early, late) for early, late in zip(back_zero, back_one)
-    )
+    results = jnp.stack([pick(back_zero[m][0], kept_one[m][0]) for m in micros])
+    results = narrow(results, members, piece)
+    sources = [[*kept_zero, *kept_one], [*back_zero, *back_one], [*starts_zero, *starts_one]]
+    sources = (
+        [[kept[at] for kept in sources[0]] for at in (2, 5, 7, 10)]
+        + [[back[at] for back in sources[1]] for at in (4, 3, 5, 6)]
+        + [sources[2]]
+    )
+    grad_gains = pick(sum(back[2] for back in back_zero), sum(back[2] for back in back_one))
     gain_terms = narrow(grad_gains, members, piece).reshape(members, 1, gain_piece)
     gain_terms = jnp.pad(gain_terms, ((0, 0), (0, 0), (0, wide - gain_piece)))
-    shares = scatter_all(
-        (normed, mixed, normed_two, normed_two, activation),
-        (grad_qkv, grad_branch, grad_gate, grad_up, grad_low),
-        gain_terms,
-        spread,
-        sizes,
-        members,
-    )
+    totals = scatter_all(sources, gain_terms, sizes, members)
+    shares = flatten_all(totals, spread, sizes)
     return (
-        results.reshape(1, micro_count, rows, model),
+        results[None],
         *shares[:4],
         shares[4][:, :gain_piece],
         *shares[5:],

time: 428 us -> 445 us (1.040)
  Pallas kernels: 342 us -> 395 us
  waiting for transfers between devices: 24.5 us -> 0.01 us
  other arithmetic: 19.7 us -> 8.52 us
    pallas_call x2 -> x4, Pallas kernels: 55.2 us -> 82.8 us  [backward_fast(): pl.pallas_call(functools.partial(backward_kernel, model, layout), grid=(h...]
    ppermute x2 -> x4, waiting for transfers between devices: 24.5 us -> 0.01 us  [passed_along(): return lax.ppermute(x, axis, pairs)]
    pallas_call x2 -> x4, Pallas kernels: 41.9 us -> 64.3 us  [forward_fast(): pl.pallas_call(functools.partial(forward_kernel, model, layout), grid=(hi...]
    select_n x7 -> x3, other arithmetic: 7.69 us -> 2.23 us  [on_device_fast(): pick = lambda early, late: jnp.where(section == 0, early, late)]
    convert_element_type x5 -> x1, other arithmetic: 4.88 us -> 0.01 us  [on_device_fast(): live[:, None].astype(jnp.bfloat16)]
    transpose x4 -> x0, local copies, waits for them, and re-layouts: 4.51 us -> none  [on_device_fast(): pick(kept_zero[at], kept_one[at])]
    unnamed x57 -> x37, local copies, waits for them, and re-layouts: 13.3 us -> 9.56 us
    pallas_call x1 -> x2, Pallas kernels: 129 us -> 133 us  [the longest x1 111 us: scatter_all(): pl.pallas_call(functools.partial(scatter_kernel, chips, sizes, micro_coun...]
  transfers between devices with their start and end apart: 2 -> 4, of which waited for: 2 -> 0; matrix products, arithmetic and copies ran while one was open for 1% -> 1% of each run, Pallas kernels for 0% -> 25%
where the time goes in v3:
time: 445 us; the launch traced here: 436 us
  Pallas kernels  395 us (89%)
  local copies, waits for them, and re-layouts  21.6 us (5%)
  other arithmetic  8.52 us (2%)
  starting transfers between devices  8.12 us (2%)
    pallas_call x1, Pallas kernels, gather_all(): pl.pallas_call(functools.partial(gather_kernel, chips, sizes), out_shape=...  115 us
    pallas_call x1, Pallas kernels, scatter_all(): pl.pallas_call(functools.partial(scatter_kernel, chips, sizes, micro_coun...  111 us
    pallas_call x4, Pallas kernels, backward_fast(): pl.pallas_call(functools.partial(backward_kernel, model, layout), grid=(h...  82.8 us
    pallas_call x4, Pallas kernels, forward_fast(): pl.pallas_call(functools.partial(forward_kernel, model, layout), grid=(hi...  64.3 us
    pallas_call x1, Pallas kernels, flatten_all(): pl.pallas_call(functools.partial(flatten_kernel, sizes), out_shape=tuple(...  21.2 us
    unnamed x37, local copies, waits for them, and re-layouts  9.56 us
  transfers between devices with their start and end apart: 4, of which 0 were waited for; matrix products, arithmetic and copies ran while one was open for 1% of the time, Pallas kernels for 25%

profile of v3, /device:TPU:0, one launch (start us, length us, event | category | flops | bytes accessed | tf_op | source)
XLA Modules:
  0.0 435.9 jit_solution(5405946078437355556)
XLA Ops:
  0.7 0.7 slice_bitcast_fusion.5
  1.6 0.6 slice.97
  2.3 0.6 slice.99
  2.9 0.7 bitcast_subtract_fusion.1
  3.8 1.4 pad_add_fusion.1
  5.4 1.3 pad_convert_fusion.1.gain_row
  6.9 0.7 copy.68.cos_table
  7.7 0.7 copy.70.late_sine
  8.4 0.7 copy.69.early_sine
  9.3 0.7 fusion.24
  10.5 1.7 fusion.spread.refs_5_
  12.2 1.1 multiply_select_fusion
  13.2 0.8 fusion.22
  14.1 115.4 %gather_ring.1 = (bf16[1024,1664]{1,0:T(8,128)(2,1)}, bf16[1024,1024]{1,0:T(8,128)(2,1)}, bf16[1024,2560]{1,0:T(8,128)(2,1)}, bf16[1024,2560]{1,0:T(8,128)(2,1)}, bf16[2560,1024]{1,0:T(8,128)(2,1)}) custom-call(bf16[1,57600]{1,0:T(2,128)(2,1)} %w_query.1, bf16[1,19200]{1,0:T(2,128)(2,1)} %w_key.1, bf16[1,19200]{1,0:T(2,128)(2,1)} %w_value.1, ...), custom_call_target="tpu_custom_call" | custom-call | tf_op jit(solution)/shard_map/gather_ring/pallas_call | solution.py:604
  129.4 0.8 slice.119
  130.3 0.7 reshape.328.gains
  131.0 16.1 %forward_layer.6 = (f32[128,1024]{1,0:T(8,128)}, bf16[128,1024]{1,0:T(8,128)(2,1)}, bf16[128,1024]{1,0:T(8,128)(2,1)}, bf16[128,1280]{1,0:T(8,128)(2,1)}, bf16[1...) custom-call(bf16[128,1024]{1,0:T(8,128)(2,1)} %get-tuple-element.192, ...), custom_call_target="tpu_custom_call" | custom-call | flops 2684354560 | bytes 29360128 | tf_op jit(solution)/shard_map/forward_layer/pallas_call | solution.py:994
  147.1 3.4 collective-permute-start.2
  150.6 0.7 copy.55.cos_table
  151.3 0.7 copy.57.late_sine
  152.0 0.7 copy.56.early_sine
  152.7 16.1 %forward_layer.4 = (f32[128,1024]{1,0:T(8,128)}, bf16[128,1024]{1,0:T(8,128)(2,1)}, bf16[128,1024]{1,0:T(8,128)(2,1)}, bf16[128,1280]{1,0:T(8,128)(2,1)}, bf16[1...) custom-call(bf16[128,1024]{1,0:T(8,128)(2,1)} %get-tuple-element.191, ...), custom_call_target="tpu_custom_call" | custom-call | flops 2684354560 | bytes 29360128 | tf_op jit(solution)/shard_map/forward_layer/pallas_call | solution.py:994
  168.8 1.5 collective-permute-start
  170.3 0.8 fusion.23
  171.2 0.7 copy-done.9
  171.9 16.1 %forward_layer.7 = (f32[128,1024]{1,0:T(8,128)}, bf16[128,1024]{1,0:T(8,128)(2,1)}, bf16[128,1024]{1,0:T(8,128)(2,1)}, bf16[128,1280]{1,0:T(8,128)(2,1)}, bf16[1...) custom-call(bf16[128,1024]{1,0:T(8,128)(2,1)} %copy-done.9, ...), custom_call_target="tpu_custom_call" | custom-call | flops 2684354560 | bytes 29360128 | tf_op jit(solution)/shard_map/forward_layer/pallas_call | solution.py:994
  187.9 20.7 %backward_layer.6 = (f32[128,1024]{1,0:T(8,128)}, bf16[128,1024]{1,0:T(8,128)(2,1)}, f32[2,1024]{1,0:T(2,128)}, bf16[128,1024]{1,0:T(8,128)(2,1)}, bf16[128,1664...) custom-call(bf16[128,1024]{1,0:T(8,128)(2,1)} %get-tuple-element.194.cotangent.refs_35_, ...), custom_call_target="tpu_custom_call" | custom-call | flops 3221225472 | bytes 31457280 | tf_op jit(solution)/shard_map/backward_layer/pallas_call | solution.py:1140
  208.6 1.7 collective-permute-start.3
  210.4 0.7 copy-done.8
  211.1 16.1 %forward_layer.5 = (f32[128,1024]{1,0:T(8,128)}, bf16[128,1024]{1,0:T(8,128)(2,1)}, bf16[128,1024]{1,0:T(8,128)(2,1)}, bf16[128,1280]{1,0:T(8,128)(2,1)}, bf16[1...) custom-call(bf16[128,1024]{1,0:T(8,128)(2,1)} %copy-done.8, ...), custom_call_target="tpu_custom_call" | custom-call | flops 2684354560 | bytes 29360128 | tf_op jit(solution)/shard_map/forward_layer/pallas_call | solution.py:994
  227.1 20.6 %backward_layer.4 = (f32[128,1024]{1,0:T(8,128)}, bf16[128,1024]{1,0:T(8,128)(2,1)}, f32[2,1024]{1,0:T(2,128)}, bf16[128,1024]{1,0:T(8,128)(2,1)}, bf16[128,1664...) custom-call(bf16[128,1024]{1,0:T(8,128)(2,1)} %get-tuple-element.193.cotangent.refs_34_, ...), custom_call_target="tpu_custom_call" | custom-call | flops 3221225472 | bytes 31457280 | tf_op jit(solution)/shard_map/backward_layer/pallas_call | solution.py:1140
  247.7 1.5 collective-permute-start.1
  249.2 0.7 copy-done.6
  249.9 20.6 %backward_layer.7 = (f32[128,1024]{1,0:T(8,128)}, bf16[128,1024]{1,0:T(8,128)(2,1)}, f32[2,1024]{1,0:T(2,128)}, bf16[128,1024]{1,0:T(8,128)(2,1)}, bf16[128,1664...) custom-call(bf16[128,1024]{1,0:T(8,128)(2,1)} %copy-done.6, ...), custom_call_target="tpu_custom_call" | custom-call | flops 3221225472 | bytes 31457280 | tf_op jit(solution)/shard_map/backward_layer/pallas_call | solution.py:1140
  270.6 1.1 broadcast_select_fusion
  271.9 0.7 copy-done.7
  272.6 20.9 %backward_layer.5 = (f32[128,1024]{1,0:T(8,128)}, bf16[128,1024]{1,0:T(8,128)(2,1)}, f32[2,1024]{1,0:T(2,128)}, bf16[128,1024]{1,0:T(8,128)(2,1)}, bf16[128,1664...) custom-call(bf16[128,1024]{1,0:T(8,128)(2,1)} %copy-done.7, ...), custom_call_target="tpu_custom_call" | custom-call | flops 3221225472 | bytes 31457280 | tf_op jit(solution)/shard_map/backward_layer/pallas_call | solution.py:1140
  293.5 1.1 broadcast_select_fusion.1
  295.0 0.8 copy.81
  295.7 1.0 copy.82
  296.9 0.7 pad.14.refs_36_
  297.6 111.4 %scatter_ring.1 = (f32[64,1664]{1,0:T(8,128)}, f32[64,1024]{1,0:T(8,128)}, f32[64,2560]{1,0:T(8,128)}, f32[64,2560]{1,0:T(8,128)}, f32[160,1024]{1,0:T(8,128)}) custom-call(bf16[128,1024]{1,0:T(8,128)(2,1)} %get-tuple-element.124.refs_0_, bf16[128,1024]{1,0:T(8,128)(2,1)} %get-tuple-element.125.refs_1_, bf16[128,1024]{1,0:T(8,128)(2,1)} %get-tuple-element.126.refs_2_, ...), custom_call_target="tpu_custom_call" | custom-call | tf_op jit(solution)/shard_map/scatter_ring/pallas_call | solution.py:767
  409.0 1.1 copy-done.1
  410.1 1.1 copy-done.2
  411.2 1.1 copy-done.3
  412.3 1.0 copy-done.4
  413.3 0.9 copy-done.5
  414.2 21.2 %flatten_pieces.1 = (f32[1,57600]{1,0:T(1,128)}, f32[1,19200]{1,0:T(1,128)}, f32[1,19200]{1,0:T(1,128)}, f32[1,57600]{1,0:T(1,128)}, f32[1,128]{1,0:T(1,128)}, /...) custom-call(f32[64,1664]{1,0:T(8,128)S(1)} %copy-done.4, f32[64,1024]{1,0:T(8,128)S(1)} %copy-done.5, ...), custom_call_target="tpu_custom_call" | custom-call | tf_op jit(solution)/shard_map/flatten_pieces/pallas_call | solution.py:822
  (67 shorter events, 2.5 us)
Async XLA Ops:
  0.6 9.3 %copy-start.12 = (bf16[1,2,128,960]{2,3,1,0:T(8,128)(2,1)S(1)}, bf16[1,2,128,960]{2,3,1,0:T(8,128)(2,1)}, u32[]{:S(2)}) copy-start(bf16[1,2,128,960]{2,3,1,0:T(8,128)(2,1)} %param.10) | copy-start | bytes 1474564
  147.1 24.1 %collective-permute-start.2 = (bf16[128,1024]{1,0:T(8,128)(2,1)}, bf16[128,1024]{1,0:T(8,128)(2,1)S(1)}, u32[]{:S(2)}, u32[]{:S(2)}) collective-permute-start(bf16[128,1024]{1,0:T(8,128)(2,1)} %get-tuple-element.110), channel_id=1, source_target_pairs={{0,16},{1,17},{2,18},{3,19},{4,20},{5,21},{6,22},{7,23},{8,24},{9,... | collective-permute-start | bytes 786440 | tf_op jit(solution)/shard_map/ppermute | solution.py:20
  168.8 41.5 %collective-permute-start = (bf16[128,1024]{1,0:T(8,128)(2,1)}, bf16[128,1024]{1,0:T(8,128)(2,1)S(1)}, u32[]{:S(2)}, u32[]{:S(2)}) collective-permute-start(bf16[128,1024]{1,0:T(8,128)(2,1)} %get-tuple-element.96), channel_id=1, source_target_pairs={{0,16},{1,17},{2,18},{3,19},{4,20},{5,21},{6,22},{7,23},{8,24},{9,... | collective-permute-start | bytes 786440 | tf_op jit(solution)/shard_map/ppermute | solution.py:20
  171.2 0.7 copy-start.9
  208.6 40.6 %collective-permute-start.3 = (bf16[128,1024]{1,0:T(8,128)(2,1)}, bf16[128,1024]{1,0:T(8,128)(2,1)S(1)}, u32[]{:S(2)}, u32[]{:S(2)}) collective-permute-start(bf16[128,1024]{1,0:T(8,128)(2,1)} %get-tuple-element.116), channel_id=1, source_target_pairs={{16,0},{17,1},{18,2},{19,3},{20,4},{21,5},{22,6},{23,7},{24,8},{25... | collective-permute-start | bytes 786440 | tf_op jit(solution)/shard_map/ppermute | solution.py:20
  210.3 0.7 copy-start.8
  247.7 24.1 %collective-permute-start.1 = (bf16[128,1024]{1,0:T(8,128)(2,1)}, bf16[128,1024]{1,0:T(8,128)(2,1)S(1)}, u32[]{:S(2)}, u32[]{:S(2)}) collective-permute-start(bf16[128,1024]{1,0:T(8,128)(2,1)} %get-tuple-element.102), channel_id=1, source_target_pairs={{16,0},{17,1},{18,2},{19,3},{20,4},{21,5},{22,6},{23,7},{24,8},{25... | collective-permute-start | bytes 786440 | tf_op jit(solution)/shard_map/ppermute | solution.py:20
  249.2 0.7 copy-start.6
  249.9 20.7 %copy-start.10 = (f32[128,1024]{1,0:T(8,128)S(1)}, f32[128,1024]{1,0:T(8,128)}, u32[]{:S(2)}) copy-start(f32[128,1024]{1,0:T(8,128)} %get-tuple-element.123) | copy-start | bytes 1572868
  271.9 0.7 copy-start.7
  272.6 20.9 %copy-start.11 = (f32[128,1024]{1,0:T(8,128)S(1)}, f32[128,1024]{1,0:T(8,128)}, u32[]{:S(2)}) copy-start(f32[128,1024]{1,0:T(8,128)} %get-tuple-element.109) | copy-start | bytes 1572868
  294.9 1.8 copy-start.13
  294.9 1.8 copy-start.14
  294.9 1.8 copy-start.15
  294.9 1.8 copy-start.16
  297.6 111.4 %copy-start = (bf16[960,1024]{1,0:T(8,128)(2,1)S(1)}, bf16[960,1024]{1,0:T(8,128)(2,1)}, u32[]{:S(2)}) copy-start(bf16[960,1024]{1,0:T(8,128)(2,1)} %fusion.spread.refs_5_) | copy-start | bytes 5898244
  409.0 1.1 copy-start.1
  410.1 1.1 copy-start.2
  411.2 1.1 copy-start.3
  412.3 1.0 copy-start.4
  413.3 0.9 copy-start.5

commit v4 on v3

--- a/solution.py
+++ b/solution.py
@@ -487,16 +487,6 @@
     pl.loop(0, count // unit)(body)
 
 
-def rows_into(flat, stage, count, width, lane):
-    unit = unit_of(width)
-
-    def body(line):
-        taken = [stage[pl.ds(line * unit + u, 1), lane : lane + width] for u in range(unit)]
-        flat[0:1, flat_part(line, width)] = jnp.concatenate(taken, axis=1)
-
-    pl.loop(0, count // unit)(body)
-
-
 SEND_ORDER = (2, 3, 4, 0, 1)
 
 
@@ -782,52 +772,6 @@
         ),
         name="scatter_ring",
     )(*flat_sources, gain_terms)
-
-
-def flatten_kernel(sizes, *refs):
-    piece, hidden_piece, model, kv_width, hidden = sizes
-    totals, spread = refs[:5], refs[5]
-    out_query, out_key, out_value, out_out, out_gains, out_gate, out_up, out_down = refs[6:14]
-    stage = refs[14]
-    rows_into(out_gate, totals[2], piece, hidden, 0)
-    rows_into(out_up, totals[3], piece, hidden, 0)
-    rows_into(out_query, totals[0], piece, model, 0)
-    rows_into(out_key, totals[0], piece, kv_width, model)
-    rows_into(out_value, totals[0], piece, kv_width, model + kv_width)
-    out_gains[...] = totals[1][piece : piece + 1, : out_gains.shape[1]]
-    for index in (1, 4):
-        total = totals[index][...]
-        upper = total.astype(jnp.bfloat16)
-        lower = (total - upper.astype(jnp.float32)).astype(jnp.bfloat16)
-        stage[: total.shape[0], :] = dot_nt(upper, spread[...]) + dot_nt(lower, spread[...])
-        if index == 1:
-            rows_into(out_out, stage, piece, model, 0)
-        else:
-            rows_into(out_down, stage, hidden_piece, model, 0)
-
-
-def flatten_all(totals, spread, sizes):
-    piece, hidden_piece, model, kv_width, hidden = sizes
-    lengths = (
-        piece * model,
-        piece * kv_width,
-        piece * kv_width,
-        piece * model,
-        -(-2 * piece // 128) * 128,
-        piece * hidden,
-        piece * hidden,
-        hidden_piece * model,
-    )
-    vmem = pl.BlockSpec(memory_space=pltpu.VMEM)
-    return pl.pallas_call(
-        functools.partial(flatten_kernel, sizes),
-        out_shape=tuple(jax.ShapeDtypeStruct((1, length), jnp.float32) for length in lengths),
-        in_specs=[vmem] * 6,
-        out_specs=tuple([vmem] * 8),
-        scratch_shapes=[pltpu.VMEM((max(totals[1].shape[0], hidden_piece), model), jnp.float32)],
-        compiler_params=pltpu.CompilerParams(vmem_limit_bytes=40 * 2**20),
-        name="flatten_pieces",
-    )(*totals, spread)
 
 
 def dot(left, right):
@@ -1001,7 +945,7 @@
         scratch_shapes=[pltpu.VMEM((tokens, heads * HEAD), low)],
         compiler_params=pltpu.CompilerParams(vmem_limit_bytes=56 * 2**20),
         cost_estimate=pl.CostEstimate(
-            flops=10 * 2**28, bytes_accessed=28 * 2**20, transcendentals=2**20
+            flops=20 * 2**28, bytes_accessed=30 * 2**20, transcendentals=2**20
         ),
         name="forward_layer",
     )(*ins, w_gate, w_up, w_down)
@@ -1153,7 +1097,7 @@
         ],
         compiler_params=pltpu.CompilerParams(vmem_limit_bytes=56 * 2**20),
         cost_estimate=pl.CostEstimate(
-            flops=12 * 2**28, bytes_accessed=30 * 2**20, transcendentals=2**20
+            flops=24 * 2**28, bytes_accessed=36 * 2**20, transcendentals=2**20
         ),
         name="backward_layer",
     )(*ins, gate_pre, up_pre, w_gate, w_up, w_down)
@@ -1239,49 +1183,39 @@
 
     own = spread_out(boundary.reshape(tokens, model))
     dimmed = jnp.where(section == 1, own * live[:, None].astype(jnp.bfloat16), 0.0)
-    alone = (heads, kv_heads, 1, rows)
-    micros = range(micro_count)
-    part = lambda array, micro: array[micro * rows : (micro + 1) * rows]
-    shared = [
-        (gain_pair, bias[m : m + 1], tuple(part(t, m) for t in tables), spread, gathered)
-        for m in micros
-    ]
-    streams_zero = [part(own, m) for m in micros]
-    kept_zero = [forward_fast(model, alone, streams_zero[m], *shared[m]) for m in micros]
-    streams_one = [passed_along(kept[1], "section", 1) for kept in kept_zero]
-    kept_one = [forward_fast(model, alone, streams_one[m], *shared[m]) for m in micros]
-    starts_one = [part(dimmed, m).astype(jnp.bfloat16) for m in micros]
-    back_one = [
-        backward_fast(model, alone, starts_one[m], (streams_one[m], *kept_one[m][1:]), *shared[m])
-        for m in micros
-    ]
-    starts_zero = [passed_along(back[1], "section", -1) for back in back_one]
-    back_zero = [
-        backward_fast(
-            model, alone, starts_zero[m], (streams_zero[m], *kept_zero[m][1:]), *shared[m]
-        )
-        for m in micros
-    ]
+    shared = (gain_pair, bias, tables, spread, gathered)
+    kept_zero = forward_fast(model, layout, own, *shared)
+    stream_one = passed_along(kept_zero[1], "section", 1)
+    kept_one = forward_fast(model, layout, stream_one, *shared)
+    start_one = dimmed.astype(jnp.bfloat16)
+    back_one = backward_fast(model, layout, start_one, (stream_one, *kept_one[1:]), *shared)
+    start_zero = passed_along(back_one[1], "section", -1)
+    back_zero = backward_fast(model, layout, start_zero, (own, *kept_zero[1:]), *shared)
 
     pick = lambda early, late: jnp.where(section == 0, early, late)
-    results = jnp.stack([pick(back_zero[m][0], kept_one[m][0]) for m in micros])
-    results = narrow(results, members, piece)
-    sources = [[*kept_zero, *kept_one], [*back_zero, *back_one], [*starts_zero, *starts_one]]
+    results = narrow(pick(back_zero[0], kept_one[0]), members, piece)
     sources = (
-        [[kept[at] for kept in sources[0]] for at in (2, 5, 7, 10)]
-        + [[back[at] for back in sources[1]] for at in (4, 3, 5, 6)]
-        + [sources[2]]
-    )
-    grad_gains = pick(sum(back[2] for back in back_zero), sum(back[2] for back in back_one))
-    gain_terms = narrow(grad_gains, members, piece).reshape(members, 1, gain_piece)
+        [(kept_zero[at], kept_one[at]) for at in (2, 5, 7, 10)]
+        + [(back_zero[at], back_one[at]) for at in (4, 3, 5, 6)]
+        + [(start_zero, start_one)]
+    )
+    gain_terms = narrow(pick(back_zero[2], back_one[2]), members, piece)
+    gain_terms = gain_terms.reshape(members, 1, gain_piece)
     gain_terms = jnp.pad(gain_terms, ((0, 0), (0, 0), (0, wide - gain_piece)))
-    totals = scatter_all(sources, gain_terms, sizes, members)
-    shares = flatten_all(totals, spread, sizes)
+    share_qkv, share_out, share_gate, share_up, share_down = scatter_all(
+        sources, gain_terms, sizes, members
+    )
+    flat = lambda array: array.reshape(1, -1)
     return (
-        results[None],
-        *shares[:4],
-        shares[4][:, :gain_piece],
-        *shares[5:],
+        results.reshape(1, micro_count, rows, model),
+        flat(share_qkv[:piece, :model]),
+        flat(share_qkv[:piece, model:split]),
+        flat(share_qkv[:piece, split : split + kv_width]),
+        flat(narrow(share_out[:piece], members, piece)),
+        flat(share_out[piece : piece + 1, :gain_piece]),
+        flat(share_gate[:piece]),
+        flat(share_up[:piece]),
+        flat(narrow(share_down, members, piece)),
     )
 
 

time: 445 us -> 408 us (0.917)
  Pallas kernels: 395 us -> 333 us
  waiting for transfers between devices: 0.01 us -> 25.9 us
    ppermute x4 -> x2, waiting for transfers between devices: 0.01 us -> 25.9 us  [passed_along(): return lax.ppermute(x, axis, pairs)]
    pallas_call x1 -> x0, Pallas kernels: 21.2 us -> none  [flatten_all(): pl.pallas_call(functools.partial(flatten_kernel, sizes), out_shape=tuple(...]
    pallas_call x4 -> x2, Pallas kernels: 82.8 us -> 62.2 us  [backward_fast(): pl.pallas_call(functools.partial(backward_kernel, model, layout), grid=(h...]
    pallas_call x4 -> x2, Pallas kernels: 64.3 us -> 44.4 us  [forward_fast(): pl.pallas_call(functools.partial(forward_kernel, model, layout), grid=(hi...]
    another operation x1 -> x4, local copies, waits for them, and re-layouts: 0.08 us -> 4.81 us  [the longest x2 4.23 us: on_device_fast(): flat = lambda array: array.reshape(1, -1)]
    unnamed x37 -> x27, local copies, waits for them, and re-layouts: 9.56 us -> 7.16 us
  transfers between devices with their start and end apart: 4 -> 2, of which waited for: 0 -> 2; matrix products, arithmetic and copies ran while one was open for 1% -> 0% of each run, Pallas kernels for 25% -> 0%
where the time goes in v4:
time: 408 us; the launch traced here: 400 us
  Pallas kernels  333 us (82%)
  waiting for transfers between devices  25.9 us (6%)
  local copies, waits for them, and re-layouts  24.8 us (6%)
  other arithmetic  7.66 us (2%)
  starting transfers between devices  5.03 us (1%)
    pallas_call x1, Pallas kernels, gather_all(): pl.pallas_call(functools.partial(gather_kernel, chips, sizes), out_shape=...  115 us
    pallas_call x1, Pallas kernels, scatter_all(): pl.pallas_call(functools.partial(scatter_kernel, chips, sizes, micro_coun...  111 us
    pallas_call x2, Pallas kernels, backward_fast(): pl.pallas_call(functools.partial(backward_kernel, model, layout), grid=(h...  62.2 us
    pallas_call x2, Pallas kernels, forward_fast(): pl.pallas_call(functools.partial(forward_kernel, model, layout), grid=(hi...  44.4 us
    ppermute x2, waiting for transfers between devices, passed_along(): return lax.ppermute(x, axis, pairs)  25.9 us
  transfers between devices with their start and end apart: 2, of which 2 were waited for; matrix products, arithmetic and copies ran while one was open for 0% of the time, Pallas kernels for 0%

profile of v4, /device:TPU:0, one launch (start us, length us, event | category | flops | bytes accessed | tf_op | source)
XLA Modules:
  0.0 400.1 jit_solution(5770726877874191664)
XLA Ops:
  0.7 0.7 slice_bitcast_fusion.3
  1.3 0.2 reduce-window.6
  1.5 0.6 slice.57
  2.1 0.2 reduce-window.9
  2.3 0.6 slice.59
  2.9 0.7 bitcast_subtract_fusion.1
  3.8 1.4 pad_add_fusion.1
  5.3 1.3 pad_convert_fusion.1.gain_row
  6.6 0.2 multiply_sine_fusion
  6.8 0.8 copy.40.cos_table
  7.7 0.8 copy.42.late_sine
  8.4 0.8 copy.41.early_sine
  9.2 1.5 copy.37
  10.7 1.6 fusion.spread
  12.4 115.4 %gather_ring.1 = (bf16[1024,1664]{1,0:T(8,128)(2,1)}, bf16[1024,1024]{1,0:T(8,128)(2,1)}, bf16[1024,2560]{1,0:T(8,128)(2,1)}, bf16[1024,2560]{1,0:T(8,128)(2,1)}, bf16[2560,1024]{1,0:T(8,128)(2,1)}) custom-call(bf16[1,57600]{1,0:T(2,128)(2,1)} %w_query.1, bf16[1,19200]{1,0:T(2,128)(2,1)} %w_key.1, bf16[1,19200]{1,0:T(2,128)(2,1)} %w_value.1, ...), custom_call_target="tpu_custom_call" | custom-call | tf_op jit(solution)/shard_map/gather_ring/pallas_call | solution.py:594
  127.7 0.8 slice.72
  128.6 0.7 reshape.251.gains
  129.3 0.8 and_select_fusion.bias
  130.1 2.0 multiply_select_fusion
  132.1 22.2 %forward_layer.2 = (f32[256,1024]{1,0:T(8,128)}, bf16[256,1024]{1,0:T(8,128)(2,1)}, bf16[256,1024]{1,0:T(8,128)(2,1)}, bf16[256,1280]{1,0:T(8,128)(2,1)}, bf16[2...) custom-call(bf16[256,1024]{1,0:T(8,128)(2,1)} %get-tuple-element.122, ...), custom_call_target="tpu_custom_call" | custom-call | flops 5368709120 | bytes 31457280 | tf_op jit(solution)/shard_map/forward_layer/pallas_call | solution.py:938
  154.3 3.7 collective-permute-start
  158.0 11.7 %collective-permute-done.stream = bf16[256,1024]{1,0:T(8,128)(2,1)S(1)} collective-permute-done((bf16[256,1024]{1,0:T(8,128)(2,1)}, bf16[256,1024]{1,0:T(8,128)(2,1)S(1)}, u32[]{:S(2)}, u32[]{:S(2)}) %collective-permute-start) | collective-permute-done | bytes 524320 | tf_op jit(solution)/shard_map/ppermute | solution.py:20
  169.7 0.8 copy-done.1
  170.5 22.2 %forward_layer.3 = (f32[256,1024]{1,0:T(8,128)}, bf16[256,1024]{1,0:T(8,128)(2,1)}, bf16[256,1024]{1,0:T(8,128)(2,1)}, bf16[256,1280]{1,0:T(8,128)(2,1)}, bf16[2...) custom-call(bf16[256,1024]{1,0:T(8,128)(2,1)} %copy-done.1, ...), custom_call_target="tpu_custom_call" | custom-call | flops 5368709120 | bytes 31457280 | tf_op jit(solution)/shard_map/forward_layer/pallas_call | solution.py:938
  192.7 26.8 %backward_layer.2 = (f32[256,1024]{1,0:T(8,128)}, bf16[256,1024]{1,0:T(8,128)(2,1)}, f32[2,1024]{1,0:T(2,128)}, bf16[256,1024]{1,0:T(8,128)(2,1)}, bf16[256,1664...) custom-call(bf16[256,1024]{1,0:T(8,128)(2,1)} %get-tuple-element.121.cotangent.refs_17_, ...), custom_call_target="tpu_custom_call" | custom-call | flops 6442450944 | bytes 37748736 | tf_op jit(solution)/shard_map/backward_layer/pallas_call | solution.py:1084
  219.5 1.3 collective-permute-start.1
  220.8 14.2 %collective-permute-done.1.cotangent.refs_16_ = bf16[256,1024]{1,0:T(8,128)(2,1)S(1)} collective-permute-done((bf16[256,1024]{1,0:T(8,128)(2,1)}, bf16[256,1024]{1,0:T(8,128)(2,1)S(1)}, u32[]{:S(2)}, u32[]{:S(2)}) %collective-permute-start.1) | collective-permute-done | bytes 524320 | tf_op jit(solution)/shard_map/ppermute | solution.py:20
  235.0 0.8 copy-done
  235.8 35.4 %backward_layer.3 = (f32[256,1024]{1,0:T(8,128)}, bf16[256,1024]{1,0:T(8,128)(2,1)}, f32[2,1024]{1,0:T(2,128)}, bf16[256,1024]{1,0:T(8,128)(2,1)}, bf16[256,1664...) custom-call(bf16[256,1024]{1,0:T(8,128)(2,1)} %copy-done, ...), custom_call_target="tpu_custom_call" | custom-call | flops 6442450944 | bytes 37748736 | tf_op jit(solution)/shard_map/backward_layer/pallas_call | solution.py:1084
  271.2 0.7 broadcast_select_fusion.1
  272.1 0.7 pad.14.refs_18_
  272.8 111.4 %scatter_ring.1 = (f32[64,1664]{1,0:T(8,128)}, f32[64,1024]{1,0:T(8,128)}, f32[64,2560]{1,0:T(8,128)}, f32[64,2560]{1,0:T(8,128)}, f32[160,1024]{1,0:T(8,128)}) custom-call(bf16[256,1024]{1,0:T(8,128)(2,1)} %get-tuple-element.70.refs_0_, bf16[256,1024]{1,0:T(8,128)(2,1)} %get-tuple-element.71.refs_1_, bf16[256,1024]{1,0:T(8,128)(2,1)} %get-tuple-element.72.refs_2_, ...), custom_call_target="tpu_custom_call" | custom-call | tf_op jit(solution)/shard_map/scatter_ring/pallas_call | solution.py:757
  384.2 1.6 fusion.20
  385.8 1.0 slice.63
  386.8 0.2 broadcast_select_fusion
  387.0 0.3 copy.52
  387.4 0.5 reshape_reshape.12
  387.9 1.0 copy.53
  389.0 1.5 copy.57
  390.4 0.5 slice.68
  390.9 1.0 reshape.244
  391.9 0.8 reshape.246
  392.7 0.8 reshape.245
  393.4 0.1 reshape.247
  393.5 1.4 reshape_reshape.14
  395.0 1.5 copy.58
  396.4 0.3 reshape.250
  396.8 2.9 reshape_reshape.15
  (44 shorter events, 0.9 us)
Async XLA Ops:
  154.3 15.4 %collective-permute-start = (bf16[256,1024]{1,0:T(8,128)(2,1)}, bf16[256,1024]{1,0:T(8,128)(2,1)S(1)}, u32[]{:S(2)}, u32[]{:S(2)}) collective-permute-start(bf16[256,1024]{1,0:T(8,128)(2,1)} %get-tuple-element.56), channel_id=1, source_target_pairs={{0,16},{1,17},{2,18},{3,19},{4,20},{5,21},{6,22},{7,23},{8,24},{9,... | collective-permute-start | bytes 1572872 | tf_op jit(solution)/shard_map/ppermute | solution.py:20
  169.7 0.8 copy-start.1
  219.5 15.5 %collective-permute-start.1 = (bf16[256,1024]{1,0:T(8,128)(2,1)}, bf16[256,1024]{1,0:T(8,128)(2,1)S(1)}, u32[]{:S(2)}, u32[]{:S(2)}) collective-permute-start(bf16[256,1024]{1,0:T(8,128)(2,1)} %get-tuple-element.62), channel_id=1, source_target_pairs={{16,0},{17,1},{18,2},{19,3},{20,4},{21,5},{22,6},{23,7},{24,8},{25... | collective-permute-start | bytes 1572872 | tf_op jit(solution)/shard_map/ppermute | solution.py:20
  235.0 0.8 copy-start
  235.8 35.4 %copy-start.9 = (f32[2,1024]{1,0:T(2,128)S(1)}, f32[2,1024]{1,0:T(2,128)}, u32[]{:S(2)}) copy-start(f32[2,1024]{1,0:T(2,128)} %get-tuple-element.87) | copy-start | bytes 24580
  272.8 114.0 %copy-start.2 = (f32[256,1024]{1,0:T(8,128)S(1)}, f32[256,1024]{1,0:T(8,128)}, u32[]{:S(2)}) copy-start(f32[256,1024]{1,0:T(8,128)} %get-tuple-element.69) | copy-start | bytes 3145732
  272.8 114.0 %copy-start.3 = (f32[256,1024]{1,0:T(8,128)S(1)}, f32[256,1024]{1,0:T(8,128)}, u32[]{:S(2)}) copy-start(f32[256,1024]{1,0:T(8,128)} %get-tuple-element.68) | copy-start | bytes 3145732
  387.0 1.9 copy-start.5
  387.9 2.5 copy-start.8
  387.9 4.0 %copy-start.7 = (f32[60,320]{1,0:T(8,128)S(1)}, f32[60,320]{1,0:T(8,128)}, u32[]{:S(2)}) copy-start(f32[60,320]{1,0:T(8,128)} %get-tuple-element.111) | copy-start | bytes 230404
  388.9 6.0 %copy-start.4 = (f32[64,2560]{1,0:T(8,128)S(1)}, f32[64,2560]{1,0:T(8,128)}, u32[]{:S(2)}) copy-start(f32[64,2560]{1,0:T(8,128)} %get-tuple-element.91) | copy-start | bytes 1966084
  390.4 6.0 %copy-start.6 = (f32[160,1024]{1,0:T(8,128)S(1)}, f32[160,1024]{1,0:T(8,128)}, u32[]{:S(2)}) copy-start(f32[160,1024]{1,0:T(8,128)} %get-tuple-element.92) | copy-start | bytes 1966084
